TPU v7x, 32 devices: a whole 2x2x4 slice. The times are simulated.
32 devices in a mesh: dp: 4 (over x, core), ty: 2 (over y), tx: 4 (over z).
Axes of the slice: x: 2, y: 2, z: 4, core: 2. Of those that a mesh axis runs over, the one named last changes fastest.
Arguments:
- features: bfloat16 [4, 12, 64, 64, 256], P('dp', None, 'ty', 'tx'), may hold values from -6 to 6
- extra_inputs: bfloat16 [4, 12, 64, 64, 9], P('dp', None, 'ty', 'tx'), may hold values from -6 to 6
- first_kernel: bfloat16 [3, 3, 265, 256], replicated, may hold values from -0.125 to 0.125
- first_bias: bfloat16 [256], replicated, may hold values from -3 to 3
- second_kernel: bfloat16 [3, 3, 256, 256], replicated, may hold values from -0.125 to 0.125
- second_bias: bfloat16 [256], replicated, may hold values from -3 to 3
- skip_kernel: bfloat16 [265, 256], replicated, may hold values from -0.375 to 0.375
- skip_bias: bfloat16 [256], replicated, may hold values from -3 to 3
- seam_table: int32 [12, 4, 4], replicated, may hold values from 0 to 11, as said below
- cotangent: bfloat16 [4, 12, 64, 64, 256], P('dp', None, 'ty', 'tx'), may hold values from -6 to 6
Outputs:
- block_output: bfloat16 [4, 12, 64, 64, 256], P('dp', None, 'ty', 'tx')
- grad_features: bfloat16 [4, 12, 64, 64, 256], P('dp', None, 'ty', 'tx')
- grad_extra: bfloat16 [4, 12, 64, 64, 9], P('dp', None, 'ty', 'tx')
- grad_first_kernel: float32 [3, 3, 265, 256], replicated
- grad_first_bias: float32 [256], replicated
- grad_second_kernel: float32 [3, 3, 256, 256], replicated
- grad_second_bias: float32 [256], replicated
- grad_skip_kernel: float32 [265, 256], replicated
- grad_skip_bias: float32 [256], replicated
Inputs may be any that keep to these rules, and one draw needn't show every extreme that they name: seam_table[f, s] holds a source face below 12, a source side below 4, a reversal flag and a corner rule, each 0 or 1; every face is a source of exactly 4 sides.
All inputs are finite; a program needn't handle non-finite values.
Results may differ from a plain program's by a relative error of at most 0.006.
Values may be sent and summed in bfloat16 or wider, within the bound.
A program may use at most 320 MiB of HBM per device.

v0:
```python
from functools import partial

import jax
import jax.numpy as jnp
from jax import lax
from jax.sharding import PartitionSpec as P


def extended(value, sides, width):
    for axis, dim in sides:
        size, length = (lax.axis_size(axis), value.shape[dim])
        up = [(i, (i + 1) % size) for i in range(size - 1)]
        down = [(j, i) for i, j in up]
        last = lax.slice_in_dim(value, length - width, length, axis=dim)
        leading = lax.slice_in_dim(value, 0, width, axis=dim)
        before = lax.ppermute(last, axis, up)
        after = lax.ppermute(leading, axis, down)
        value = jnp.concatenate([before, value, after], axis=dim)
    return value


def face_lines(edge_rows, seam_table):
    face_hot = (
        seam_table[:, :, 0][:, :, None]
        == jnp.arange(edge_rows.shape[1], dtype=jnp.int32)[None, None, :]
    ).astype(edge_rows.dtype)
    side_hot = (
        seam_table[:, :, 1][:, :, None] == jnp.arange(4, dtype=jnp.int32)[None, None, :]
    ).astype(edge_rows.dtype)
    chooser = face_hot[:, :, :, None] * side_hot[:, :, None, :]
    side_lines = jnp.einsum(
        "fsgt,bgtnc->bfsnc",
        chooser,
        edge_rows,
        precision=lax.Precision.HIGHEST,
        preferred_element_type=jnp.float32,
    ).astype(edge_rows.dtype)
    flipped = seam_table[:, :, 2][None, :, :, None, None] == 1
    side_lines = jnp.where(flipped, side_lines[:, :, :, ::-1, :], side_lines)
    corner_rule = seam_table[:, :, 3][None, :, :, None] == 0
    upper_line = side_lines[:, :, 0]
    right_line = side_lines[:, :, 1]
    lower_line = side_lines[:, :, 2]
    left_line = side_lines[:, :, 3]
    upper_left = jnp.where(corner_rule[:, :, 0], upper_line[:, :, 0], left_line[:, :, 0])
    upper_right = jnp.where(corner_rule[:, :, 1], upper_line[:, :, -1], right_line[:, :, 0])
    lower_right = jnp.where(corner_rule[:, :, 2], lower_line[:, :, -1], right_line[:, :, -1])
    lower_left = jnp.where(corner_rule[:, :, 3], lower_line[:, :, 0], left_line[:, :, -1])
    upper_full = jnp.concatenate(
        [upper_left[:, :, None], upper_line, upper_right[:, :, None]], axis=2
    )
    right_full = jnp.concatenate(
        [upper_right[:, :, None], right_line, lower_right[:, :, None]], axis=2
    )
    lower_full = jnp.concatenate(
        [lower_left[:, :, None], lower_line, lower_right[:, :, None]], axis=2
    )
    left_full = jnp.concatenate([upper_left[:, :, None], left_line, lower_left[:, :, None]], axis=2)
    return (upper_full, right_full, lower_full, left_full)


def seam_layer(edge_rows, seam_table, place):
    row_index, column_index, row_count, column_count, tile_rows, tile_columns = place
    upper_full, right_full, lower_full, left_full = face_lines(edge_rows, seam_table)
    upper_piece = lax.dynamic_slice_in_dim(
        upper_full, column_index * tile_columns, tile_columns + 2, 2
    )
    lower_piece = lax.dynamic_slice_in_dim(
        lower_full, column_index * tile_columns, tile_columns + 2, 2
    )
    left_piece = lax.dynamic_slice_in_dim(left_full, row_index * tile_rows, tile_rows + 2, 2)
    right_piece = lax.dynamic_slice_in_dim(right_full, row_index * tile_rows, tile_rows + 2, 2)
    grid_rows = lax.broadcasted_iota(jnp.int32, (tile_rows + 2, tile_columns + 2, 1), 0)
    grid_columns = lax.broadcasted_iota(jnp.int32, (tile_rows + 2, tile_columns + 2, 1), 1)
    seam_cells = jnp.zeros(
        upper_piece.shape[:2] + (tile_rows + 2, tile_columns + 2, upper_piece.shape[-1]),
        edge_rows.dtype,
    )
    seam_cells = jnp.where((grid_rows == 0) & (row_index == 0), upper_piece[:, :, None], seam_cells)
    seam_cells = jnp.where(
        (grid_rows == tile_rows + 1) & (row_index == row_count - 1),
        lower_piece[:, :, None],
        seam_cells,
    )
    seam_cells = jnp.where(
        (grid_columns == 0) & (column_index == 0), left_piece[:, :, :, None], seam_cells
    )
    seam_cells = jnp.where(
        (grid_columns == tile_columns + 1) & (column_index == column_count - 1),
        right_piece[:, :, :, None],
        seam_cells,
    )
    return seam_cells


def join_tiles(tile_parts):
    moved = jnp.moveaxis(tile_parts, 0, 2)
    return moved.reshape(
        tile_parts.shape[1],
        tile_parts.shape[2],
        tile_parts.shape[0] * tile_parts.shape[3],
        tile_parts.shape[4],
    )


def face_edges(field):
    row_count = lax.axis_size("ty")
    column_count = lax.axis_size("tx")
    row_edges = jnp.stack([field[:, :, 0], field[:, :, -1]], axis=2)
    column_edges = jnp.stack([field[:, :, :, -1], field[:, :, :, 0]], axis=2)
    row_gathered, column_gathered = (
        lax.all_gather(row_edges[None], ("ty", "tx"), axis=0, tiled=True),
        lax.all_gather(column_edges[None], ("ty", "tx"), axis=0, tiled=True),
    )
    row_grid = row_gathered.reshape((row_count, column_count) + row_edges.shape)
    column_grid = column_gathered.reshape((row_count, column_count) + column_edges.shape)
    upper_edge = join_tiles(row_grid[0, :, :, :, 0])
    lower_edge = join_tiles(row_grid[row_count - 1, :, :, :, 1])
    right_edge = join_tiles(column_grid[:, column_count - 1, :, :, 0])
    left_edge = join_tiles(column_grid[:, 0, :, :, 1])
    return jnp.stack([upper_edge, right_edge, lower_edge, left_edge], axis=2)


def extend(field, seam_table, place):
    rimmed = extended(field, (("ty", 2), ("tx", 3)), 1)
    return rimmed + seam_layer(face_edges(field), seam_table, place)


def collect(grad_padded, seam_table, place):
    row_index, column_index, row_count, column_count, tile_rows, tile_columns = place
    widened = extended(grad_padded.astype(jnp.bfloat16), (("ty", 2), ("tx", 3)), 1).astype(
        grad_padded.dtype
    )
    inside = grad_padded[:, :, 1:-1, 1:-1]
    inside = inside.at[:, :, 0].add(widened[:, :, 0, 2 : tile_columns + 2])
    inside = inside.at[:, :, -1].add(widened[:, :, tile_rows + 3, 2 : tile_columns + 2])
    inside = inside.at[:, :, :, 0].add(widened[:, :, 2 : tile_rows + 2, 0])
    inside = inside.at[:, :, :, -1].add(widened[:, :, 2 : tile_rows + 2, tile_columns + 3])
    inside = inside.at[:, :, 0, 0].add(widened[:, :, 0, 0])
    inside = inside.at[:, :, 0, -1].add(widened[:, :, 0, tile_columns + 3])
    inside = inside.at[:, :, -1, 0].add(widened[:, :, tile_rows + 3, 0])
    inside = inside.at[:, :, -1, -1].add(widened[:, :, tile_rows + 3, tile_columns + 3])
    blank = jnp.zeros(
        grad_padded.shape[:2] + (4, tile_rows * row_count, grad_padded.shape[-1]), jnp.float32
    )
    unused, seam_pull = jax.vjp(
        lambda edge_values: seam_layer(edge_values, seam_table, place), blank
    )
    (edge_grads,) = seam_pull(grad_padded)
    edge_grads = lax.psum(edge_grads, ("ty", "tx"))
    upper_part = lax.dynamic_slice_in_dim(
        edge_grads[:, :, 0], column_index * tile_columns, tile_columns, 2
    )
    right_part = lax.dynamic_slice_in_dim(edge_grads[:, :, 1], row_index * tile_rows, tile_rows, 2)
    lower_part = lax.dynamic_slice_in_dim(
        edge_grads[:, :, 2], column_index * tile_columns, tile_columns, 2
    )
    left_part = lax.dynamic_slice_in_dim(edge_grads[:, :, 3], row_index * tile_rows, tile_rows, 2)
    inside = inside.at[:, :, 0].add(jnp.where(row_index == 0, upper_part, 0.0))
    inside = inside.at[:, :, -1].add(jnp.where(row_index == row_count - 1, lower_part, 0.0))
    inside = inside.at[:, :, :, 0].add(jnp.where(column_index == 0, left_part, 0.0))
    inside = inside.at[:, :, :, -1].add(
        jnp.where(column_index == column_count - 1, right_part, 0.0)
    )
    return inside


def conv_valid(padded, kernel):
    shape_in = padded.shape
    merged = padded.reshape(shape_in[0] * shape_in[1], shape_in[2], shape_in[3], shape_in[4])
    result = lax.conv_general_dilated(
        merged,
        kernel,
        (1, 1),
        "VALID",
        dimension_numbers=("NHWC", "HWIO", "NHWC"),
        preferred_element_type=jnp.float32,
    )
    return result.reshape(
        shape_in[0], shape_in[1], shape_in[2] - 2, shape_in[3] - 2, kernel.shape[-1]
    )


def conv_back(grad_pre, kernel):
    flipped = jnp.transpose(kernel[::-1, ::-1], (0, 1, 3, 2))
    surround = jnp.pad(grad_pre, ((0, 0), (0, 0), (2, 2), (2, 2), (0, 0)))
    return conv_valid(surround, flipped)


def kernel_grad(padded, grad_pre):
    tile_rows = grad_pre.shape[2]
    tile_columns = grad_pre.shape[3]
    pieces = []
    for offset_row in range(3):
        for offset_column in range(3):
            window = padded[
                :,
                :,
                offset_row : offset_row + tile_rows,
                offset_column : offset_column + tile_columns,
            ]
            pieces.append(
                jnp.einsum("sfhwc,sfhwd->cd", window, grad_pre, preferred_element_type=jnp.float32)
            )
    return jnp.stack(pieces).reshape(3, 3, padded.shape[-1], grad_pre.shape[-1])


def per_device(
    features,
    extra_inputs,
    first_kernel,
    first_bias,
    second_kernel,
    second_bias,
    skip_kernel,
    skip_bias,
    seam_table,
    cotangent,
):
    place = (
        lax.axis_index("ty"),
        lax.axis_index("tx"),
        lax.axis_size("ty"),
        lax.axis_size("tx"),
        features.shape[2],
        features.shape[3],
    )
    gelu_exact = partial(jax.nn.gelu, approximate=False)
    joined = jnp.concatenate([features, extra_inputs], axis=-1)
    padded_one = extend(joined, seam_table, place)
    pre_one = conv_valid(padded_one, first_kernel) + first_bias
    active_one, slope_one = jax.vjp(gelu_exact, pre_one)
    hidden = active_one.astype(jnp.bfloat16)
    padded_two = extend(hidden, seam_table, place)
    pre_two = conv_valid(padded_two, second_kernel) + second_bias
    active_two, slope_two = jax.vjp(gelu_exact, pre_two)
    skipped = (
        jnp.einsum("sfhwc,cd->sfhwd", joined, skip_kernel, preferred_element_type=jnp.float32)
        + skip_bias
    )
    block_output = (active_two + skipped).astype(jnp.bfloat16)
    (grad_two,) = slope_two(cotangent.astype(jnp.float32))
    grad_two = grad_two.astype(jnp.bfloat16)
    second_kernel_grad = kernel_grad(padded_two, grad_two)
    second_bias_grad = jnp.sum(grad_two, axis=(0, 1, 2, 3), dtype=jnp.float32)
    grad_hidden = collect(conv_back(grad_two, second_kernel), seam_table, place)
    (grad_one,) = slope_one(grad_hidden)
    grad_one = grad_one.astype(jnp.bfloat16)
    first_kernel_grad = kernel_grad(padded_one, grad_one)
    first_bias_grad = jnp.sum(grad_one, axis=(0, 1, 2, 3), dtype=jnp.float32)
    grad_joined = collect(conv_back(grad_one, first_kernel), seam_table, place)
    grad_joined = grad_joined + jnp.einsum(
        "sfhwd,cd->sfhwc", cotangent, skip_kernel, preferred_element_type=jnp.float32
    )
    skip_kernel_grad = jnp.einsum(
        "sfhwc,sfhwd->cd", joined, cotangent, preferred_element_type=jnp.float32
    )
    skip_bias_grad = jnp.sum(cotangent, axis=(0, 1, 2, 3), dtype=jnp.float32)
    summed = lax.psum(
        (
            first_kernel_grad,
            first_bias_grad,
            second_kernel_grad,
            second_bias_grad,
            skip_kernel_grad,
            skip_bias_grad,
        ),
        ("dp", "ty", "tx"),
    )
    grad_joined = grad_joined.astype(jnp.bfloat16)
    channels = features.shape[-1]
    return (
        block_output,
        grad_joined[..., :channels],
        grad_joined[..., channels:],
        summed[0],
        summed[1],
        summed[2],
        summed[3],
        summed[4],
        summed[5],
    )


def solution(mesh):
    return jax.shard_map(
        per_device,
        mesh=mesh,
        in_specs=(
            P("dp", None, "ty", "tx", None),
            P("dp", None, "ty", "tx", None),
            P(),
            P(),
            P(),
            P(),
            P(),
            P(),
            P(),
            P("dp", None, "ty", "tx", None),
        ),
        out_specs=(
            P("dp", None, "ty", "tx", None),
            P("dp", None, "ty", "tx", None),
            P("dp", None, "ty", "tx", None),
            P(),
            P(),
            P(),
            P(),
            P(),
            P(),
        ),
        check_vma=False,
    )
```

profile of v0, /device:TPU:0, one launch (start us, length us, event | category | flops | bytes accessed | tf_op | source)
XLA Modules:
  0.0 1239.2 jit_solution(1524706134377364010)
XLA Ops:
  54.9 13.8 %all-gather.9.cloned.1.call-done = bf16[8,12,2,16,265]{4,3,2,1,0:T(8,128)(2,1)} async-done(((bf16[1,12,2,16,265]{4,3,2,1,0:T(8,128)(2,1)}), bf16[8,12,2,16,265]{4,3,2,1,0:T(8,128)(2,1)}) %all-gather.9.cloned.1.call-update) | async-done | bytes 1628176 | tf_op jit(solution)/shard_map/all_gather | solution.py:112
  72.1 80.3 %all-gather.11.cloned.1.call-done = bf16[8,12,2,32,265]{4,3,2,1,0:T(8,128)(2,1)} async-done(((bf16[1,12,2,32,265]{4,3,2,1,0:T(8,128)(2,1)}), bf16[8,12,2,32,265]{4,3,2,1,0:T(8,128)(2,1)}) %all-gather.11.cloned.1.call-update) | async-done | bytes 3256336 | tf_op jit(solution)/shard_map/all_gather | solution.py:113
  160.0 10.5 maximum_add_fusion
  170.6 210.8 %fusion.26 = f32[12,32,16,256]{3,0,2,1:T(8,128)S(1)} fusion(bf16[3,3,265,256]{3,2,1,0:T(8,128)(2,1)S(1)} %copy-done, bf16[12,34,18,265]{3,2,1,0:T(8,128)(2,1)S(1)} %maximum_add_fusion), kind=kOutput, calls=%fused_computation.73 | convolution fusion | flops 7502561280 | bytes 11404896 | tf_op jit(solution)/shard_map/conv_general_dilated | solution.py:171
  381.4 19.4 %fusion.63 = (bf16[1,12,32,16,256]{4,1,3,2,0:T(8,128)(2,1)S(1)}, f32[12,32,16,256]{3,0,2,1:T(8,128)}) fusion(f32[12,32,16,256]{3,0,2,1:T(8,128)S(1)} %fusion.26, f32[256]{0:T(256)S(1)} %convert_element_type.132), kind=kLoop, calls=%fused_computation.132 | loop fusion | flops 103809024 | bytes 15729664 | tf_op jit(solution)/shard_map/convert_element_type | solution.py:233
  428.7 15.8 %maximum_add_fusion.1 = bf16[1,12,34,18,265]{4,3,2,1,0:T(8,128)(2,1)} fusion(bf16[1,12,34,1,265]{4,3,2,1,0:T(2,128)(2,1)S(1)} %copy.306, bf16[1,12,1,16,265]{4,3,2,1,0:T(8,128)(2,1)S(1)} %copy-done.37, bf16[1,12,32,16,9]{4,3,2,1,0:T(8,128)(2,1)S(1)} %copy.251, bf16[1,12,32,16,256]{4,3,2,1,0:T(8,128)(2,1)S(1)} %copy-done.2, ...), kind=kLoop, calls=%fused_computation.72 | loop fusion | flops 35030880 | bytes 8446184 | tf_op jit(solution)/shard_map/add | solution.py:126
  455.2 54.7 %all-gather.15.cloned.1.call-done = bf16[8,12,2,32,256]{4,3,2,1,0:T(8,128)(2,1)} async-done(((bf16[1,12,2,32,256]{4,3,2,1,0:T(8,128)(2,1)}), bf16[8,12,2,32,256]{4,3,2,1,0:T(8,128)(2,1)}) %all-gather.15.cloned.1.call-update) | async-done | bytes 3145744 | tf_op jit(solution)/shard_map/all_gather | solution.py:113
  515.4 36.5 %convert_reduce_fusion.1 = (f32[256]{0:T(256)}, bf16[1,12,32,16,256]{4,1,3,2,0:T(8,128)(2,1)S(1)}, f32[12,32,16,256]{3,0,2,1:T(8,128)}, f32[256]{0:T(256)}, f32[12,32,16,256]{3,0,2,1:T(8,128)}) fusion(bf16[1,12,32,16,256]{4,3,2,1,0:T(8,128)(2,1)S(1)} %copy-done.9, f32[256]{0:T(256)S(1)} %copy-done.82, bf16[3,3,256,256]{3,2,1,0:T(8,128)(2,1)S(1)} %copy-done.86, ...), kind=kOutput, calls=%fused_computation.41 | convolution fusion | flops 7382028288 | bytes 24456296 | tf_op jit(solution)/shard_map/conv_general_dilated | solution.py:171
  551.9 20.2 %select_reduce_fusion.6 = (f32[12,18,256]{2,0,1:T(8,128)S(1)}, f32[12,18,256]{2,0,1:T(8,128)S(1)}, f32[12,34,256]{2,0,1:T(8,128)S(1)}, f32[12,34,256]{2,0,1:T(8,128)S(1)}, f32[12,34,18,256]{3,0,2,1:T(8,128)}) fusion(pred[34]{0:T(512)(128)(4,1)S(1)} %copy-done.57, pred[18]{0:T(512)(128)(4,1)S(1)} %copy-done.60, pred[18]{0:T(512)(128)(4,1)S(1)} %copy-done.63, ...), kind=kOutput, calls=%fused_computation.14 | convolution fusion | flops 8683696128 | bytes 13123688 | tf_op jit(solution)/shard_map/conv_general_dilated | solution.py:171
  602.4 9.8 slice_bitcast_fusion.18
  645.5 8.9 fusion.64
  654.4 7.9 fusion.187
  673.4 9.8 copy.495
  686.0 8.1 slice.1314
  708.7 39.4 %all-reduce.32.cloned.1.call-done = f32[1,12,4,64,256]{4,1,2,3,0:T(8,128)} async-done(((f32[1,12,4,64,256]{4,1,2,3,0:T(8,128)}), f32[1,12,4,64,256]{4,1,2,3,0:T(8,128)}) %all-reduce.32.cloned.1.call-update) | async-done | bytes 3145744 | tf_op jit(solution)/shard_map/psum | solution.py:150
  756.5 8.2 copy.293
  776.1 26.4 %fusion.33 = f32[12,34,18,265]{3,0,2,1:T(8,128)} fusion(bf16[3,3,265,256]{3,2,1,0:T(8,128)(2,1)S(1)} %copy-done, bf16[1,12,32,16,256]{4,1,3,2,0:T(8,128)(2,1)S(1)} %get-tuple-element.351), kind=kOutput, calls=%fused_computation.84 | convolution fusion | flops 8967905280 | bytes 12151488 | tf_op jit(solution)/shard_map/conv_general_dilated | solution.py:171
  802.5 9.1 convert_bitcast_fusion
  811.6 22.0 %select_reduce_fusion.2 = (f32[12,18,265]{2,1,0:T(8,128)S(1)}, f32[12,18,265]{2,1,0:T(8,128)S(1)}, f32[12,34,265]{2,1,0:T(8,128)S(1)}, f32[12,34,265]{2,1,0:T(8,128)S(1)}) fusion(f32[12,34,18,265]{3,0,2,1:T(8,128)} %fusion.33, pred[34]{0:T(512)(128)(4,1)S(1)} %copy-done.57, pred[18]{0:T(512)(128)(4,1)S(1)} %copy-done.60, pred[18]{0:T(512)(128)(4,1)S(1)} %copy-done.63, ...), kind=kLoop, calls=%fused_computation.2 | loop fusion | flops 21077040 | bytes 9107624 | tf_op jit(solution)/shard_map/transpose(jvp(jit(_where)))/reduce_sum | solution.py:80
  844.6 7.5 fusion.97
  878.8 11.5 slice.1332
  891.0 42.4 %all-reduce.26 = (f32[256]{0:T(256)}, f32[256]{0:T(256)}, f32[256]{0:T(256)}) all-reduce(f32[256]{0:T(256)S(1)} %copy-done.77, f32[256]{0:T(256)S(1)} %copy-done.84, f32[256]{0:T(256)S(1)} %copy-done.85), channel_id=1, replica_groups=mesh['dp'=4,'ty'=2,'tx'=4] {'dp','ty','tx'}, use_global_device_ids=true, to_apply=%region_13.14 | all-reduce | flops 768 | bytes 6144 | tf_op jit(solution)/shard_map/psum | solution.py:259
  949.2 123.1 %all-reduce.34.cloned.1.call-done = f32[1,12,4,64,265]{4,1,3,2,0:T(8,128)} async-done(((f32[1,12,4,64,265]{4,1,3,2,0:T(8,128)}), f32[1,12,4,64,265]{4,1,3,2,0:T(8,128)}) %all-reduce.34.cloned.1.call-update) | async-done | bytes 3256336 | tf_op jit(solution)/shard_map/psum | solution.py:150
  1093.3 133.2 %all-reduce.36.cloned.1.call-done = (f32[3,3,265,256]{3,2,1,0:T(8,128)}, f32[3,3,256,256]{3,2,1,0:T(8,128)}, f32[265,256]{1,0:T(8,128)}) async-done(((f32[3,3,265,256]{3,2,1,0:T(8,128)}, f32[3,3,256,256]{3,2,1,0:T(8,128)}, f32[265,256]{1,0:T(8,128)}), (f32[3,3,265,256]{3,2,1,0:T(8,128)}, f32[3,3,256,256]{3,2,1,0:T(8,128)}, f32[265,256]{1,0:T(8,128)})) %all-reduce.36.cloned.1.call-update) | async-done | bytes 5072912 | tf_op jit(solution)/shard_map/psum | solution.py:259
  (437 shorter events, 293.1 us)
Async XLA Ops:
  7.2 61.4 %all-gather.9.cloned.1.call-start = ((), (), s32[]{:S(2)}) async-start(), calls=%async_computation.2 | async-start | bytes 2654208 | tf_op jit(solution)/shard_map/all_gather | solution.py:112
  11.7 140.6 %all-gather.11.cloned.1.call-start = ((), (), s32[]{:S(2)}) async-start(), calls=%async_computation.3 | async-start | bytes 5308416 | tf_op jit(solution)/shard_map/all_gather | solution.py:113
  15.7 438.0 %all-gather.13.cloned.1.call-start = ((), (), s32[]{:S(2)}) async-start(), calls=%async_computation.4 | async-start | bytes 1769472 | tf_op jit(solution)/shard_map/all_gather | solution.py:112
  15.7 8.1 collective-permute-start.1
  17.0 11.0 collective-permute-start
  23.3 561.7 %copy-start.51 = (pred[12,4,1]{0,1,2:T(4,128)(4,1)}, pred[12,4,1]{0,1,2:T(4,128)(4,1)S(1)}, u32[]{:S(2)}) copy-start(pred[12,4,1]{0,1,2:T(4,128)(4,1)S(1)} %copy.503) | copy-start | bytes 148
  34.2 11.6 collective-permute-start.3
  35.6 17.2 %collective-permute-start.2 = (bf16[1,12,34,1,265]{4,2,3,1,0:T(8,128)(2,1)S(1)}, bf16[1,12,34,1,265]{4,2,3,1,0:T(8,128)(2,1)S(1)}, u32[]{:S(2)}, u32[]{:S(2)}) collective-permute-start(bf16[1,12,34,1,265]{4,2,3,1,0:T(8,128)(2,1)S(1)} %copy.252), channel_id=1, source_target_pairs={{0,1},{1,2},{2,3},{4,5},{5,6},{6,7},{8,9},{9,10},{10,11},{12,13},{... | collective-permute-start | bytes 648728 | tf_op jit(solution)/shard_map/ppermute | solution.py:16
  404.3 105.7 %all-gather.15.cloned.1.call-start = ((), (), s32[]{:S(2)}) async-start(), calls=%async_computation.5 | async-start | bytes 3538944 | tf_op jit(solution)/shard_map/all_gather | solution.py:113
  415.7 332.5 %all-reduce.32.cloned.1.call-start = ((), (), s32[]{:S(2)}) async-start(), calls=%async_computation | async-start | bytes 8388608 | tf_op jit(solution)/shard_map/psum | solution.py:150
  422.4 22.0 %collective-permute-start.5 = (bf16[1,12,1,16,256]{4,1,3,2,0:T(8,128)(2,1)S(1)}, bf16[1,12,1,16,256]{4,1,3,2,0:T(8,128)(2,1)S(1)}, u32[]{:S(2)}, u32[]{:S(2)}) collective-permute-start(bf16[1,12,1,16,256]{4,1,3,2,0:T(8,128)(2,1)S(1)} %copy-done.47), channel_id=1, source_target_pairs={{4,0},{5,1},{6,2},{7,3},{12,8},{13,9},{14,10},{15,11},{20,16},{21,... | collective-permute-start | bytes 294920 | tf_op jit(solution)/shard_map/ppermute | solution.py:17
  424.0 20.5 %collective-permute-start.4 = (bf16[1,12,1,16,256]{4,1,3,2,0:T(8,128)(2,1)S(1)}, bf16[1,12,1,16,256]{4,1,3,2,0:T(8,128)(2,1)S(1)}, u32[]{:S(2)}, u32[]{:S(2)}) collective-permute-start(bf16[1,12,1,16,256]{4,1,3,2,0:T(8,128)(2,1)S(1)} %get-tuple-element.395), channel_id=1, source_target_pairs={{0,4},{1,5},{2,6},{3,7},{8,12},{9,13},{10,14},{11,15},{16,20},{17,... | collective-permute-start | bytes 294920 | tf_op jit(solution)/shard_map/ppermute | solution.py:16
  447.8 66.5 %collective-permute-start.7 = (bf16[1,12,34,1,256]{4,1,3,2,0:T(8,128)(2,1)}, bf16[1,12,34,1,256]{4,1,3,2,0:T(8,128)(2,1)S(1)}, u32[]{:S(2)}, u32[]{:S(2)}) collective-permute-start(bf16[1,12,34,1,256]{4,1,3,2,0:T(8,128)(2,1)} %get-tuple-element.386), channel_id=1, source_target_pairs={{1,0},{2,1},{3,2},{5,4},{6,5},{7,6},{9,8},{10,9},{11,10},{13,12},{... | collective-permute-start | bytes 626696 | tf_op jit(solution)/shard_map/ppermute | solution.py:17
  449.1 65.3 %collective-permute-start.6 = (bf16[1,12,34,1,256]{4,1,3,2,0:T(8,128)(2,1)S(1)}, bf16[1,12,34,1,256]{4,1,3,2,0:T(8,128)(2,1)S(1)}, u32[]{:S(2)}, u32[]{:S(2)}) collective-permute-start(bf16[1,12,34,1,256]{4,1,3,2,0:T(8,128)(2,1)S(1)} %get-tuple-element.385), channel_id=1, source_target_pairs={{0,1},{1,2},{2,3},{4,5},{5,6},{6,7},{8,9},{9,10},{10,11},{12,13},{... | collective-permute-start | bytes 626696 | tf_op jit(solution)/shard_map/ppermute | solution.py:16
  577.4 84.9 %collective-permute-start.9 = (bf16[1,12,1,18,256]{4,1,2,3,0:T(8,128)(2,1)}, bf16[1,12,1,18,256]{4,1,2,3,0:T(8,128)(2,1)S(1)}, u32[]{:S(2)}, u32[]{:S(2)}) collective-permute-start(bf16[1,12,1,18,256]{4,1,2,3,0:T(8,128)(2,1)} %get-tuple-element.374), channel_id=1, source_target_pairs={{4,0},{5,1},{6,2},{7,3},{12,8},{13,9},{14,10},{15,11},{20,16},{21,... | collective-permute-start | bytes 331784 | tf_op jit(solution)/shard_map/ppermute | solution.py:17
  578.6 83.7 %collective-permute-start.8 = (bf16[1,12,1,18,256]{4,1,2,3,0:T(8,128)(2,1)S(1)}, bf16[1,12,1,18,256]{4,1,2,3,0:T(8,128)(2,1)S(1)}, u32[]{:S(2)}, u32[]{:S(2)}) collective-permute-start(bf16[1,12,1,18,256]{4,1,2,3,0:T(8,128)(2,1)S(1)} %get-tuple-element.373), channel_id=1, source_target_pairs={{0,4},{1,5},{2,6},{3,7},{8,12},{9,13},{10,14},{11,15},{16,20},{17,... | collective-permute-start | bytes 331784 | tf_op jit(solution)/shard_map/ppermute | solution.py:16
  591.5 480.8 %all-reduce.34.cloned.1.call-start = ((), (), s32[]{:S(2)}) async-start(), calls=%async_computation.1 | async-start | bytes 12582912 | tf_op jit(solution)/shard_map/psum | solution.py:150
  662.4 31.7 %collective-permute-start.11 = (bf16[1,12,36,1,256]{4,1,2,3,0:T(8,128)(2,1)S(1)}, bf16[1,12,36,1,256]{4,1,2,3,0:T(8,128)(2,1)S(1)}, u32[]{:S(2)}, u32[]{:S(2)}) collective-permute-start(bf16[1,12,36,1,256]{4,1,2,3,0:T(8,128)(2,1)S(1)} %get-tuple-element.363), channel_id=1, source_target_pairs={{1,0},{2,1},{3,2},{5,4},{6,5},{7,6},{9,8},{10,9},{11,10},{13,12},{... | collective-permute-start | bytes 663560 | tf_op jit(solution)/shard_map/ppermute | solution.py:17
  664.0 30.2 %collective-permute-start.10 = (bf16[1,12,36,1,256]{4,1,2,3,0:T(8,128)(2,1)S(1)}, bf16[1,12,36,1,256]{4,1,2,3,0:T(8,128)(2,1)S(1)}, u32[]{:S(2)}, u32[]{:S(2)}) collective-permute-start(bf16[1,12,36,1,256]{4,1,2,3,0:T(8,128)(2,1)S(1)} %get-tuple-element.362), channel_id=1, source_target_pairs={{0,1},{1,2},{2,3},{4,5},{5,6},{6,7},{8,9},{9,10},{10,11},{12,13},{... | collective-permute-start | bytes 663560 | tf_op jit(solution)/shard_map/ppermute | solution.py:16
  834.8 35.6 %collective-permute-start.13 = (bf16[1,12,1,18,265]{4,1,3,2,0:T(8,128)(2,1)S(1)}, bf16[1,12,1,18,265]{4,1,3,2,0:T(8,128)(2,1)S(1)}, u32[]{:S(2)}, u32[]{:S(2)}) collective-permute-start(bf16[1,12,1,18,265]{4,1,3,2,0:T(8,128)(2,1)S(1)} %get-tuple-element.357), channel_id=1, source_target_pairs={{4,0},{5,1},{6,2},{7,3},{12,8},{13,9},{14,10},{15,11},{20,16},{21,... | collective-permute-start | bytes 343448 | tf_op jit(solution)/shard_map/ppermute | solution.py:17
  836.1 34.3 %collective-permute-start.12 = (bf16[1,12,1,18,265]{4,1,3,2,0:T(8,128)(2,1)S(1)}, bf16[1,12,1,18,265]{4,1,3,2,0:T(8,128)(2,1)S(1)}, u32[]{:S(2)}, u32[]{:S(2)}) collective-permute-start(bf16[1,12,1,18,265]{4,1,3,2,0:T(8,128)(2,1)S(1)} %get-tuple-element.356), channel_id=1, source_target_pairs={{0,4},{1,5},{2,6},{3,7},{8,12},{9,13},{10,14},{11,15},{16,20},{17,... | collective-permute-start | bytes 343448 | tf_op jit(solution)/shard_map/ppermute | solution.py:16
  852.1 374.4 %all-reduce.36.cloned.1.call-start = ((), (), s32[]{:S(2)}) async-start(), calls=%async_computation.6 | async-start | bytes 10289152 | tf_op jit(solution)/shard_map/psum | solution.py:259
  871.4 61.9 %collective-permute-start.15 = (bf16[1,12,36,1,265]{4,1,3,2,0:T(8,128)(2,1)S(1)}, bf16[1,12,36,1,265]{4,1,3,2,0:T(8,128)(2,1)S(1)}, u32[]{:S(2)}, u32[]{:S(2)}) collective-permute-start(bf16[1,12,36,1,265]{4,1,3,2,0:T(8,128)(2,1)S(1)} %get-tuple-element.355), channel_id=1, source_target_pairs={{1,0},{2,1},{3,2},{5,4},{6,5},{7,6},{9,8},{10,9},{11,10},{13,12},{... | collective-permute-start | bytes 686888 | tf_op jit(solution)/shard_map/ppermute | solution.py:17
  872.7 60.6 %collective-permute-start.14 = (bf16[1,12,36,1,265]{4,1,3,2,0:T(8,128)(2,1)S(1)}, bf16[1,12,36,1,265]{4,1,3,2,0:T(8,128)(2,1)S(1)}, u32[]{:S(2)}, u32[]{:S(2)}) collective-permute-start(bf16[1,12,36,1,265]{4,1,3,2,0:T(8,128)(2,1)S(1)} %get-tuple-element.354), channel_id=1, source_target_pairs={{0,1},{1,2},{2,3},{4,5},{5,6},{6,7},{8,9},{9,10},{10,11},{12,13},{... | collective-permute-start | bytes 686888 | tf_op jit(solution)/shard_map/ppermute | solution.py:16
  (107 other events, 2340.0 us)
Sparse Core Ops, SparseCore 0:
  11.8 56.7 all-gather.8
  70.7 81.5 all-gather.10
  404.4 42.0 all-gather.12
  449.1 60.8 all-gather.14
  591.6 156.5 all-reduce.31
  852.2 220.0 all-reduce.33
  1079.9 146.5 all-reduce.35
where the time goes:
time: 1240 us
  waiting for transfers between devices  459 us (37%)
  matrix products  389 us (31%)
  other arithmetic  159 us (13%)
  local copies, waits for them, and re-layouts  125 us (10%)
  starting transfers between devices  49.4 us (4%)
  blocking collectives  42.4 us (3%)
  between operations  16.5 us (1%)
    conv_general_dilated x4, matrix products, conv_valid(): lax.conv_general_dilated(merged, kernel, (1, 1), 'VALID', dimension_numbe...  294 us
    psum x2, waiting for transfers between devices, collect(): edge_grads = lax.psum(edge_grads, ('ty', 'tx'))  163 us
    all_gather x2, waiting for transfers between devices, face_edges(): lax.all_gather(column_edges[None], ('ty', 'tx'), axis=0, tiled=True)  135 us
    psum x1, waiting for transfers between devices, per_device(): lax.psum((first_kernel_grad, first_bias_grad, second_kernel_grad, second_...  133 us
    dot_general x18, matrix products, kernel_grad(): jnp.einsum('sfhwc,sfhwd->cd', window, grad_pre, preferred_element_type=jn...  60.2 us
    psum x1, blocking collectives, per_device(): lax.psum((first_kernel_grad, first_bias_grad, second_kernel_grad, second_...  42.4 us
    ppermute x8, starting transfers between devices, extended(): before = lax.ppermute(last, axis, up)  37.7 us
    unnamed x231, local copies, waits for them, and re-layouts  35.8 us
  transfers between devices with their start and end apart: 23, of which 10 were waited for; matrix products, arithmetic and copies ran while one was open for 20% of the time, Pallas kernels for 0%

commit v1 on v0

--- a/solution.py
+++ b/solution.py
@@ -3,6 +3,8 @@
 import jax
 import jax.numpy as jnp
 from jax import lax
+from jax.experimental import pallas as pl
+from jax.experimental.pallas import tpu as pltpu
 from jax.sharding import PartitionSpec as P
 
 
@@ -282,9 +284,1036 @@
     )
 
 
+TAPS = 9
+SUM_ROWS = 2560
+LANES = 128
+PACK = 27
+ONE = 27
+
+
+def whole_block(
+    x_in, ext_in, w1_in, w2_in, skip_in, biases, table, cot_in,
+    out_ref, gx_ref, gext_ref, suma_ref, sumb_ref,
+    w1, w2, wskip, we, wse, sel_t, rule,
+    xv, ev, cv, t27, xc, hc, pre, slope, slev, sleh, cev, ceh,
+    ost, ff, evf, ehf, rvf, rhf, cvf, chf, rc1v, rc1h, rc2v, rc2h, gev, geh,
+    acca, accb, outa, landa, bufs, ssem, rsem, sum_ssem, sum_rsem, credit, ack, lsem,
+):
+    f32, bf = jnp.float32, jnp.bfloat16
+    dp, ty, tx = lax.axis_index("dp"), lax.axis_index("ty"), lax.axis_index("tx")
+    core, xx, place = dp % 2, dp // 2, ty * 4 + tx
+    core_mate, x_mate = dp + 1 - 2 * core, dp + 2 - 4 * xx
+    faces, rows, cols = x_in.shape[0], x_in.shape[1], x_in.shape[2]
+    area = rows * cols
+    is_mid = jnp.where((tx == 0) | (tx == 3), 0, 1)
+    hx = jnp.where(tx >= 2, 1, 0)
+    kk = ty + 2 * hx
+    mm = kk + 4 * is_mid
+    at_end = is_mid == 0
+
+    def dev(y, x):
+        return {"ty": y, "tx": x}
+
+    def rows16(start, size):
+        return pl.ds(pl.multiple_of(start, 16), size)
+
+    def home(m):
+        half = (m // 2) % 2
+        return m % 2, (3 * half if m // 4 == 0 else 1 + half)
+
+    def home_class(k):
+        half = k // 2
+        return k % 2, jnp.where(at_end, 3 * half, 1 + half)
+
+    def flip48(flag, k, n):
+        return 48 * jnp.where(flag, n - 1 - k, k)
+
+    class Exchange:
+        def __init__(self, index):
+            self.index = index
+            self.ed_v, self.ed_h, self.db, self.sb, self.rg_v, self.rg_h, self.rg_c, self.xw, self.xd = bufs[index]
+            self.sent = []
+            self.slot = 0
+
+        def send(self, cond, src, dst, rs, target):
+            copy = pltpu.make_async_remote_copy(
+                src_ref=src, dst_ref=dst, send_sem=ssem.at[self.index, self.slot],
+                recv_sem=rsem.at[self.index, rs], device_id=target, device_id_type=pl.DeviceIdType.MESH,
+            )
+            self.slot += 1
+            self.sent.append((cond, copy))
+            if cond is None:
+                copy.start()
+            else:
+                pl.when(cond)(copy.start)
+
+        def get(self, cond, dst, rs):
+            copy = pltpu.make_async_remote_copy(
+                src_ref=dst, dst_ref=dst, send_sem=ssem.at[self.index, 0],
+                recv_sem=rsem.at[self.index, rs], device_id=dev(1 - ty, tx), device_id_type=pl.DeviceIdType.MESH,
+            )
+            if cond is None:
+                copy.wait_recv()
+            else:
+                pl.when(cond)(copy.wait_recv)
+
+        def drain(self):
+            for cond, copy in self.sent:
+                if cond is None:
+                    copy.wait_send()
+                else:
+                    pl.when(cond)(copy.wait_send)
+
+        def move(self, cond, dst, dst_at, src, src_at):
+            @pl.when(cond)
+            def _():
+                dst[dst_at] = src[src_at]
+
+    class Forward(Exchange):
+        def start(self):
+            ed_v, ed_h, db = self.ed_v, self.ed_h, self.db
+            for k in range(4):
+                at = rows16(flip48(hx == 1, k, 4), 48)
+                to = rows16((2 * ty) * 96 + hx * 48, 48)
+                y, x = home_class(k)
+                self.send(kk != k, ed_v.at[ty, at], db.at[to], (2 * ty) * 2 + hx, dev(y, x))
+                self.move(kk == k, db, (to,), ed_v, (ty, at))
+            for m in range(8):
+                at = rows16(flip48(ty == 1, m, 8), 48)
+                side = jnp.where(hx == 1, 1, 3)
+                to = rows16(side * 96 + ty * 48, 48)
+                y, x = home(m)
+                self.send(at_end & (mm != m), ed_h.at[hx, at], db.at[to], side * 2 + ty, dev(y, x))
+                self.move(at_end & (mm == m), db, (to,), ed_h, (hx, at))
+            rg_v, rg_h, rg_c = self.rg_v, self.rg_h, self.rg_c
+            self.send(None, ed_v.at[1 - ty], rg_v.at[ty], 24, dev(1 - ty, tx))
+            self.send(tx < 3, ed_h.at[1], rg_h.at[0], 25, dev(ty, tx + 1))
+            self.send(tx > 0, ed_h.at[0], rg_h.at[1], 26, dev(ty, tx - 1))
+            self.send(tx < 3, ed_v.at[1 - ty, pl.ds(176, 16)], rg_c.at[2 * ty], 20 + 2 * ty, dev(1 - ty, tx + 1))
+            self.send(tx > 0, ed_v.at[1 - ty, pl.ds(0, 16)], rg_c.at[2 * ty + 1], 21 + 2 * ty, dev(1 - ty, tx - 1))
+
+        def middle(self):
+            db, sb = self.db, self.sb
+            for t in range(4):
+                for h in range(2):
+                    if t % 2 == 0:
+                        own = (ty == t // 2) & (hx == h)
+                    else:
+                        own = at_end & (ty == h) & (tx == (0 if t == 3 else 3))
+                    self.get(jnp.logical_not(own), db.at[pl.ds(t * 96 + h * 48, 48)], t * 2 + h)
+            sb[...] = dot_tn(sel_t[...], db[...]).astype(bf)
+            for y in range(2):
+                for h in range(2):
+                    x = jnp.where(at_end, 3 * h, 1 + h)
+                    own = (ty == y) & (tx == x)
+                    at = pl.ds(2 * y * 96 + h * 48, 48)
+                    to = rows16(48 * ((3 - kk) if h else kk), 48)
+                    self.send(jnp.logical_not(own), sb.at[at], self.rg_v.at[y, to], 8 + kk, dev(y, x))
+                    self.move(own, self.rg_v, (y, to), sb, (at,))
+            for y in range(2):
+                for h in range(2):
+                    own = (ty == y) & (tx == 3 * h)
+                    at = pl.ds((1 if h else 3) * 96 + y * 48, 48)
+                    to = rows16(48 * ((7 - mm) if y else mm), 48)
+                    self.send(jnp.logical_not(own), sb.at[at], self.rg_h.at[h, to], 12 + mm, dev(y, 3 * h))
+                    self.move(own, self.rg_h, (h, to), sb, (at,))
+            for y in range(2):
+                for m, x, right, at in ((3, 1, 0, 32), (3, 2, 1, 48), (4, 3, 0, 80), (4, 0, 1, 0), (7, 2, 0, 32), (7, 1, 1, 48)):
+                    spot = 2 * y + right
+                    src = (pl.ds(2 * y * 96 + at, 16),)
+                    if home(m) == (y, x):
+                        self.move(mm == m, self.rg_c, (spot,), sb, src)
+                    else:
+                        self.send(mm == m, sb.at[src], self.rg_c.at[spot], 20 + spot, dev(y, x))
+                for h in range(2):
+                    spot = 2 * (1 - y) + h
+                    src = pl.ds((1 if h else 3) * 96 + (32 if y else 48), 16)
+                    self.send(mm == 7, sb.at[src], self.rg_c.at[spot], 20 + spot, dev(y, 3 * h))
+
+        def finish(self):
+            self.get(None, self.rg_v.at[1 - ty], 24)
+            self.get(tx > 0, self.rg_h.at[0], 25)
+            self.get(tx < 3, self.rg_h.at[1], 26)
+            for k in range(4):
+                self.get(kk != k, self.rg_v.at[ty, rows16(flip48(hx == 1, k, 4), 48)], 8 + k)
+            for m in range(8):
+                self.get(at_end & (mm != m), self.rg_h.at[hx, rows16(flip48(ty == 1, m, 8), 48)], 12 + m)
+            for spot in range(4):
+                y, right = spot // 2, spot % 2
+                face_corner = (ty == y) & (tx == 3 * right)
+                if spot == 2:
+                    own = (ty == 1) & (tx == 2)
+                    skip = face_corner | own
+                else:
+                    skip = face_corner
+                self.get(jnp.logical_not(skip), self.rg_c.at[spot], 20 + spot)
+
+    class Backward(Exchange):
+        def start(self):
+            rg_v, rg_h, rg_c, sb, xw, xd = self.rg_v, self.rg_h, self.rg_c, self.sb, self.xw, self.xd
+            for k in range(4):
+                at = rows16(flip48(hx == 1, k, 4), 48)
+                to = rows16((2 * ty) * 96 + hx * 48, 48)
+                y, x = home_class(k)
+                self.send(kk != k, rg_v.at[ty, at], sb.at[to], (2 * ty) * 2 + hx, dev(y, x))
+                self.move(kk == k, sb, (to,), rg_v, (ty, at))
+            for m in range(8):
+                at = rows16(flip48(ty == 1, m, 8), 48)
+                side = jnp.where(hx == 1, 1, 3)
+                to = rows16(side * 96 + ty * 48, 48)
+                y, x = home(m)
+                self.send(at_end & (mm != m), rg_h.at[hx, at], sb.at[to], side * 2 + ty, dev(y, x))
+                self.move(at_end & (mm == m), sb, (to,), rg_h, (hx, at))
+            for right in range(2):
+                spot = 2 * ty + right
+                away = (tx < 3) if right else (tx > 0)
+                if right:
+                    x, y = jnp.where(tx == 0, 1, jnp.where(tx == 1, 2, 3)), jnp.where(tx == 0, 0, 1)
+                else:
+                    x, y = jnp.where(tx == 1, 3, jnp.where(tx == 2, 2, 1)), jnp.where(tx == 3, 0, 1)
+                own = away & (ty == y) & (tx == x)
+                slot = ty * 2 + right
+                self.send(away & jnp.logical_not(own), rg_c.at[spot], xw.at[slot], 8 + slot, dev(y, x))
+                self.move(own, xw, (slot,), rg_c, (spot,))
+                inner = 2 * (1 - ty) + right
+                edge = (tx == 3) if right else (tx == 0)
+                self.send(edge, rg_c.at[inner], xw.at[4 + ty * 2 + right], 12 + ty * 2 + right, dev(1, 2))
+                self.send(away, rg_c.at[inner], xd.at[1 - right], 16 + 1 - right, dev(1 - ty, tx + (1 if right else -1)))
+            ed_v, ed_h = self.ed_v, self.ed_h
+            self.send(None, rg_v.at[1 - ty], ed_v.at[ty], 30, dev(1 - ty, tx))
+            self.send(tx < 3, rg_h.at[1], ed_h.at[0], 31, dev(ty, tx + 1))
+            self.send(tx > 0, rg_h.at[0], ed_h.at[1], 32, dev(ty, tx - 1))
+
+        def middle(self):
+            sb, db, xw = self.sb, self.db, self.xw
+            for s in range(4):
+                for h in range(2):
+                    if s % 2 == 0:
+                        own = (ty == s // 2) & (hx == h)
+                    else:
+                        own = at_end & (ty == h) & (tx == (0 if s == 3 else 3))
+                    self.get(jnp.logical_not(own), sb.at[pl.ds(s * 96 + h * 48, 48)], s * 2 + h)
+            for y in range(2):
+                for right in range(2):
+                    slot = 2 * y + right
+                    wants = (mm == 3) | (mm == 4) | (mm == 7)
+                    if slot == 2:
+                        wants = (mm == 3) | (mm == 4)
+                    self.get(wants, xw.at[slot], 8 + slot)
+                    self.get(mm == 7, xw.at[4 + slot], 12 + slot)
+                    for m, at in ((3, 48 if right else 32), (4, 0 if right else 80), (7, 48 if right else 32)):
+                        @pl.when(mm == m)
+                        def _(spot=2 * y * 96 + at, slot=slot):
+                            here = pl.ds(spot, 16)
+                            sb[here] = (sb[here].astype(f32) + xw[slot].astype(f32)).astype(bf)
+
+                    @pl.when(mm == 7)
+                    def _(spot=(1 if right else 3) * 96 + (32 if y else 48), slot=4 + slot):
+                        here = pl.ds(spot, 16)
+                        sb[here] = (sb[here].astype(f32) + xw[slot].astype(f32)).astype(bf)
+            db[...] = dot(sel_t[...], sb[...]).astype(bf)
+            for y in range(2):
+                for h in range(2):
+                    x = jnp.where(at_end, 3 * h, 1 + h)
+                    own = (ty == y) & (tx == x)
+                    at = pl.ds(2 * y * 96 + h * 48, 48)
+                    to = rows16(48 * ((3 - kk) if h else kk), 48)
+                    self.send(jnp.logical_not(own), db.at[at], self.ed_v.at[y, to], 18 + kk, dev(y, x))
+                    self.move(own, self.ed_v, (y, to), db, (at,))
+            for y in range(2):
+                for h in range(2):
+                    own = (ty == y) & (tx == 3 * h)
+                    at = pl.ds((1 if h else 3) * 96 + y * 48, 48)
+                    to = rows16(48 * ((7 - mm) if y else mm), 48)
+                    self.send(jnp.logical_not(own), db.at[at], self.ed_h.at[h, to], 22 + mm, dev(y, 3 * h))
+                    self.move(own, self.ed_h, (h, to), db, (at,))
+
+        def finish(self):
+            self.get(None, self.ed_v.at[1 - ty], 30)
+            self.get(tx > 0, self.ed_h.at[0], 31)
+            self.get(tx < 3, self.ed_h.at[1], 32)
+            self.get(tx > 0, self.xd.at[0], 16)
+            self.get(tx < 3, self.xd.at[1], 17)
+            for k in range(4):
+                self.get(kk != k, self.ed_v.at[ty, rows16(flip48(hx == 1, k, 4), 48)], 18 + k)
+            for m in range(8):
+                self.get(at_end & (mm != m), self.ed_h.at[hx, rows16(flip48(ty == 1, m, 8), 48)], 22 + m)
+
+        def stage(self, blocks):
+            for j in range(blocks):
+                lanes = slice(128 * j, 128 * j + 128)
+                for s in range(2):
+                    evf[j, s] = self.ed_v[s, :, lanes].astype(f32)
+                    ehf[j, s] = self.ed_h[s, :, lanes].astype(f32)
+
+                @pl.when(tx > 0)
+                def _(j=j, lanes=lanes):
+                    evf[j, 1 - ty, pl.ds(0, 16)] += self.xd[0, :, lanes].astype(f32)
+
+                @pl.when(tx < 3)
+                def _(j=j, lanes=lanes):
+                    evf[j, 1 - ty, pl.ds(176, 16)] += self.xd[1, :, lanes].astype(f32)
+
+    class Total:
+        def __init__(self, index, acc, out, out0, land, land0):
+            self.index, self.acc, self.out, self.land = index, acc, out, land
+            self.out0, self.land0 = out0, land0
+            self.half = SUM_ROWS // 2 * core
+            self.other_half = SUM_ROWS // 2 * (1 - core)
+            self.quarter = self.half + SUM_ROWS // 4 * xx
+            self.other_quarter = self.half + SUM_ROWS // 4 * (1 - xx)
+            self.own = self.quarter + SUM_ROWS // 32 * place
+
+        def copy(self, slot, src, dst, rslot, target):
+            return pltpu.make_async_remote_copy(
+                src_ref=src, dst_ref=dst, send_sem=sum_ssem.at[self.index, slot],
+                recv_sem=sum_rsem.at[self.index, rslot], device_id=target, device_id_type=pl.DeviceIdType.MESH,
+            )
+
+        def outs(self, start, size):
+            return self.out.at[rows16(self.out0 + start, size)]
+
+        def lands(self, start, size):
+            return self.land.at[rows16(self.land0 + start, size)]
+
+        def cast(self, start, size):
+            step = SUM_ROWS // 32
+
+            @pl.loop(0, size // step)
+            def _(i):
+                at = start + i * step
+                self.out[rows16(self.out0 + at, step)] = self.acc[rows16(at, step)].astype(bf)
+
+        def add(self, start, size, land):
+            step = SUM_ROWS // 32
+
+            @pl.loop(0, size // step)
+            def _(i):
+                self.acc[rows16(start + i * step, step)] += self.land[
+                    rows16(self.land0 + land + i * step, step)].astype(f32)
+
+        def to_core(self):
+            if self.index:
+                pl.semaphore_wait(credit.at[0], 1)
+            size = SUM_ROWS // 2
+            self.cast(self.other_half, size)
+            self.first = self.copy(0, self.outs(self.other_half, size), self.lands(0, size), 0, {"dp": core_mate})
+            self.first.start()
+
+        def to_x(self):
+            if self.index:
+                pl.semaphore_wait(credit.at[1], 1)
+            self.first.wait()
+            pl.semaphore_signal(ack.at[self.index, 0], inc=1, device_id={"dp": core_mate}, device_id_type=pl.DeviceIdType.MESH)
+            size = SUM_ROWS // 4
+            self.add(self.half, SUM_ROWS // 2, 0)
+            self.cast(self.other_quarter, size)
+            self.second = self.copy(
+                1, self.outs(self.other_quarter, size), self.lands(SUM_ROWS // 2, size), 1, {"dp": x_mate})
+            self.second.start()
+
+        def peers(self):
+            for q in range(8):
+                yield q, place != q, {"ty": q // 4, "tx": q % 4}
+
+        def to_group(self):
+            if self.index:
+                pl.semaphore_wait(credit.at[2], 7)
+            self.second.wait()
+            size, step = SUM_ROWS // 4, SUM_ROWS // 32
+            self.add(self.quarter, size, SUM_ROWS // 2)
+
+            @pl.loop(0, 8)
+            def _(q):
+                here = self.acc[rows16(self.quarter + step * q, step)]
+                self.land[rows16(self.land0 + step * q, step)] = here.astype(bf)
+
+            pl.semaphore_signal(ack.at[self.index, 1], inc=1, device_id={"dp": x_mate}, device_id_type=pl.DeviceIdType.MESH)
+            self.third = []
+            base = SUM_ROWS // 4 * 3
+            for q, cond, target in self.peers():
+                copy = self.copy(2 + q, self.lands(step * q, step), self.lands(base + step * place, step), 2 + place, target)
+                pl.when(cond)(copy.start)
+                self.third.append((cond, copy))
+
+        def got(self, slot, dst):
+            return self.copy(slot, dst, dst, slot, {"dp": core_mate})
+
+        def from_group(self):
+            step, base = SUM_ROWS // 32, SUM_ROWS // 4 * 3
+            for q, cond, _ in self.peers():
+                pl.when(cond)(self.got(2 + q, self.lands(base + step * q, step)).wait_recv)
+            for q, cond, _ in self.peers():
+                @pl.when(cond)
+                def _(q=q):
+                    self.acc[rows16(self.own, step)] += self.land[rows16(self.land0 + base + step * q, step)].astype(f32)
+            for cond, copy in self.third:
+                pl.when(cond)(copy.wait_send)
+            self.cast(self.own, step)
+            self.fourth = []
+            for q, cond, target in self.peers():
+                copy = self.copy(10 + q, self.outs(self.own, step), self.outs(self.own, step), 10 + place, target)
+                pl.when(cond)(copy.start)
+                self.fourth.append((cond, copy))
+
+        def back_x(self):
+            step = SUM_ROWS // 32
+            for q, cond, _ in self.peers():
+                pl.when(cond)(self.got(10 + q, self.outs(self.quarter + step * q, step)).wait_recv)
+            size = SUM_ROWS // 4
+            pl.semaphore_wait(ack.at[self.index, 1], 1)
+            self.fifth = self.copy(18, self.outs(self.quarter, size), self.outs(self.quarter, size), 18, {"dp": x_mate})
+            self.fifth.start()
+
+        def back_core(self):
+            self.got(18, self.outs(self.other_quarter, SUM_ROWS // 4)).wait_recv()
+            size = SUM_ROWS // 2
+            pl.semaphore_wait(ack.at[self.index, 0], 1)
+            self.sixth = self.copy(19, self.outs(self.half, size), self.outs(self.half, size), 19, {"dp": core_mate})
+            self.sixth.start()
+
+        def finish(self, ref, sem):
+            self.got(19, self.outs(self.other_half, SUM_ROWS // 2)).wait_recv()
+            for cond, copy in self.fourth:
+                pl.when(cond)(copy.wait_send)
+            self.fifth.wait_send()
+            self.sixth.wait_send()
+            self.store = pltpu.make_async_copy(self.outs(0, SUM_ROWS), ref, lsem.at[sem])
+            self.store.start()
+
+    def dot(a, b):
+        return jnp.dot(a, b, preferred_element_type=f32)
+
+    def dot_nt(a, b):
+        return lax.dot_general(a, b, (((1,), (1,)), ((), ())), preferred_element_type=f32)
+
+    def dot_tn(a, b):
+        return lax.dot_general(a, b, (((0,), (0,)), ((), ())), preferred_element_type=f32)
+
+    def cat(parts, axis=-1):
+        return jnp.concatenate(parts, axis=axis)
+
+    def face_rows(f):
+        return pl.ds(pl.multiple_of(f * area, area), area)
+
+    def top(f, s):
+        return pl.ds(f * area + (area - cols if s else 0), cols)
+
+    def side(f, s):
+        return pl.ds(f * area + (cols - 1 if s else 0), rows, stride=cols)
+
+    def ring_v(f):
+        return pl.ds(f, cols, stride=faces)
+
+    def ring_h(f):
+        return pl.ds(f, rows, stride=faces)
+
+    def shifts(v):
+        zero = jnp.zeros((rows, 1, v.shape[-1]), v.dtype)
+        return cat([zero, v[:, : cols - 1]], 1), cat([v[:, 1:], zero], 1)
+
+    def fill(ref, v):
+        left, right = shifts(v)
+        wide = v.shape[-1]
+        ref[1 : rows + 1, :, 0:wide] = left
+        ref[1 : rows + 1, :, wide : 2 * wide] = v
+        ref[1 : rows + 1, :, 2 * wide : 3 * wide] = right
+
+    def windows(ref):
+        return [ref[a : a + rows].reshape(area, ref.shape[-1]) for a in range(3)]
+
+    def split(ref, at, v):
+        for h in range(2):
+            ref[(h,) + at] = v[:, 128 * h : 128 * h + 128]
+
+    def join(ref, at, blocks=2):
+        return cat([ref[(h,) + at] for h in range(blocks)])
+
+    def gelu_slope(u):
+        phi = 0.5 + 0.5 * lax.erf(u * 0.7071067811865476)
+        return u * phi, phi + u * (0.3989422804014327 * jnp.exp(-0.5 * u * u))
+
+    lane = lax.broadcasted_iota(jnp.int32, (1, LANES), 1)
+
+    first, second = Forward(0), Forward(1)
+    third, fourth = Backward(2), Backward(3)
+    def load(src, dst, sem):
+        copy = pltpu.make_async_copy(src, dst, lsem.at[sem])
+        copy.start()
+        return copy
+
+    eload, xload = load(ext_in, ev, 1), load(x_in, xv, 0)
+    w1load, skipload = load(w1_in, w1, 5), load(skip_in, wskip, 6)
+    cload, w2load = load(cot_in, cv, 2), load(w2_in, w2, 7)
+    barrier = pltpu.get_barrier_semaphore()
+    for e in (0, 1):
+        bufs[e][6][...] = jnp.zeros_like(bufs[e][6])
+    for y in range(2):
+        for x in range(4):
+            @pl.when((ty != y) | (tx != x))
+            def _(y=y, x=x):
+                pl.semaphore_signal(barrier, inc=1, device_id=dev(y, x), device_id_type=pl.DeviceIdType.MESH)
+    for mate in (core_mate, x_mate):
+        pl.semaphore_signal(barrier, inc=1, device_id={"dp": mate}, device_id_type=pl.DeviceIdType.MESH)
+    pl.semaphore_wait(barrier, 9)
+
+    for ref in (xc[0], xc[1]):
+        ref[0] = jnp.zeros(ref.shape[1:], bf)
+        ref[rows + 1] = jnp.zeros(ref.shape[1:], bf)
+
+    @pl.loop(0, faces)
+    def _(f):
+        hc[f, 0] = jnp.zeros(hc.shape[2:], bf)
+        hc[f, rows + 1] = jnp.zeros(hc.shape[2:], bf)
+        t27[f, 0] = jnp.zeros(t27.shape[2:], bf)
+        t27[f, rows + 1] = jnp.zeros(t27.shape[2:], bf)
+
+    count, span = 9 * cols, cols * LANES
+    eload.wait()
+    turned = cat([ev[f].astype(f32).reshape(count, rows).T for f in range(faces)], 0).astype(bf)
+
+    def packing(moves):
+        line = lax.broadcasted_iota(jnp.int32, (count, span), 0)
+        spot = lax.broadcasted_iota(jnp.int32, (count, span), 1)
+        channel, column, to_column, to_lane = line // cols, line % cols, spot // LANES, spot % LANES
+        hot = jnp.zeros((count, span), f32)
+        for start, step in moves:
+            hot = hot + jnp.where((to_lane == start + channel) & (column == to_column + step), 1.0, 0.0)
+        return hot.astype(bf)
+
+    flat = dot(turned, packing([(0, -1), (9, 0), (18, 1)]))
+    for c in range(cols):
+        pre[0, pl.ds(c * faces * rows, faces * rows)] = flat[:, c * LANES : c * LANES + LANES]
+    xload.wait()
+
+    @pl.loop(0, faces)
+    def _(f):
+        for c in range(cols):
+            ff[2, pl.ds(c, rows, stride=cols)] = pre[0, pl.ds(c * faces * rows + f * rows, rows)]
+        packed = ff[2] + jnp.where(lane == ONE, 1.0, 0.0)
+        t27[f, 1 : rows + 1] = packed.astype(bf).reshape(rows, cols, LANES)
+        ff[2] = jnp.where(lane < 9, pltpu.roll(packed, LANES - 9, axis=1), 0.0)
+        for h in range(2):
+            ff[h] = xv[f, :, :, 128 * h : 128 * h + 128].astype(f32).reshape(area, LANES)
+        for j in range(3):
+            for s in range(2):
+                evf[j, s, ring_v(f)] = ff[j, pl.ds(area - cols if s else 0, cols)]
+                ehf[j, s, ring_h(f)] = ff[j, pl.ds(cols - 1 if s else 0, rows, stride=cols)]
+
+    def edges_out(ex, blocks):
+        for s in range(2):
+            ex.ed_v[s] = join(evf, (s,), blocks).astype(bf)
+            ex.ed_h[s] = join(ehf, (s,), blocks).astype(bf)
+
+    edges_out(first, 3)
+    first.start()
+
+    acca[...] = jnp.zeros_like(acca)
+    accb[...] = jnp.zeros_like(accb)
+    w1load.wait()
+    skipload.wait()
+    ff[...] = jnp.zeros_like(ff)
+    for h in range(2):
+        lanes = slice(128 * h, 128 * h + 128)
+        for a in range(3):
+            for b in range(3):
+                ff[h, pl.ds(128 * a + 9 * b, 9)] = w1[3 * a + b, 256:265, lanes].astype(f32)
+        ff[h, pl.ds(128 + ONE, 1)] = biases[0:1, lanes].astype(f32)
+        ff[h, pl.ds(384 + 9, 9)] = wskip[256:265, lanes].astype(f32)
+        ff[h, pl.ds(384 + ONE, 1)] = biases[2:3, lanes].astype(f32)
+        for a in range(3):
+            we[a, :, lanes] = ff[h, pl.ds(128 * a, 128)].astype(bf)
+        wse[:, lanes] = ff[h, pl.ds(384, 128)].astype(bf)
+    total = 32 * faces
+    spread = jnp.where(
+        lax.broadcasted_iota(jnp.int32, (faces, total), 1) % faces
+        == lax.broadcasted_iota(jnp.int32, (faces, total), 0), 1.0, 0.0)
+    spot = lax.broadcasted_iota(jnp.int32, (1, total), 1)
+    side_of, step_of = spot // (8 * faces), (spot // faces % 8).astype(f32)
+    source = jnp.zeros((1, total), f32)
+    for s in range(4):
+        entry = dot(table[s].astype(f32), spread)
+        step = jnp.where(entry[2:3] > 0.5, 7.0 - step_of, step_of)
+        source = source + jnp.where(side_of == s, (entry[1:2] * 8.0 + step) * faces + entry[0:1], 0.0)
+    sel_t[...] = jnp.where(
+        lax.broadcasted_iota(jnp.int32, (total, total), 0) == source.astype(jnp.int32), 1.0, 0.0).astype(bf)
+    same = jnp.where(
+        lax.broadcasted_iota(jnp.int32, (faces, faces), 1) == lax.broadcasted_iota(jnp.int32, (faces, faces), 0), 1.0, 0.0)
+    for spot_index, k in enumerate((0, 1, 3, 2)):
+        column = jnp.sum(same * table[k, 3:4].astype(f32), axis=1, keepdims=True)
+        rule[spot_index, 0:faces] = jnp.broadcast_to(1.0 - column, (faces, LANES))
+
+    def ring_in(ex, blocks):
+        for j in range(blocks):
+            lanes = slice(128 * j, 128 * j + 128)
+            for s in range(2):
+                rvf[j, s, pl.ds(12, 192)] = ex.rg_v[s, :, lanes].astype(f32)
+                rhf[j, s, pl.ds(12, 384)] = ex.rg_h[s, :, lanes].astype(f32)
+            for spot in range(4):
+                s, right = spot // 2, spot % 2
+                win = ex.rg_c[spot, :, lanes].astype(f32)
+                edge = (tx == 3) if right else (tx == 0)
+                late = jnp.where(edge, ty == 1, right == 0)
+                got = jnp.where(late, win[4:16], win[0:12])
+                from_v = rvf[j, s, pl.ds(192 if right else 12, 12)]
+                from_h = rhf[j, right, pl.ds(384 if s else 12, 12)]
+                local = jnp.where(rule[spot, 0:12] > 0.0, from_v, from_h)
+                rvf[j, s, pl.ds(204 if right else 0, 12)] = jnp.where((ty == s) & edge, local, got)
+
+    def ring_cat(rcv, rch, blocks):
+        for s in range(2):
+            for b in range(3):
+                for j in range(2):
+                    at = slice(256 * b + 128 * j, 256 * b + 128 * j + 128)
+                    rcv[s, :, at] = rvf[j, s, pl.ds(12 * b, 192)].astype(bf)
+                    rch[s, :, at] = rhf[j, s, pl.ds(12 * b, 384)].astype(bf)
+            if blocks == 3:
+                total = rvf[2, s, pl.ds(0, 192)]
+                for b in (1, 2):
+                    total = total + pltpu.roll(rvf[2, s, pl.ds(12 * b, 192)], 9 * b, axis=1)
+                rcv[s, :, 768:896] = total.astype(bf)
+                for a in range(3):
+                    line = rhf[2, s, pl.ds(12 * a, 384)]
+                    line = pltpu.roll(line, 18, axis=1) if s else line
+                    rch[s, :, 768 + 128 * a : 896 + 128 * a] = line.astype(bf)
+
+    def zero_h_ends(blocks):
+        for j in range(blocks):
+            for s in range(2):
+                rhf[j, s, pl.ds(0, 12)] = jnp.zeros((12, LANES), f32)
+                rhf[j, s, pl.ds(396, 12)] = jnp.zeros((12, LANES), f32)
+
+    zero_h_ends(3)
+
+    def add_to_edges(source_v, source_h):
+        @pl.loop(0, faces)
+        def _(f):
+            for h in range(2):
+                for s in range(2):
+                    pre[h, top(f, s)] += source_v[h, s, ring_v(f)]
+            for h in range(2):
+                for s in range(2):
+                    pre[h, side(f, s)] += source_h[h, s, ring_h(f)]
+            for h in range(2):
+                for s in range(2):
+                    evf[h, s, ring_v(f)] = pre[h, top(f, s)]
+                    ehf[h, s, ring_h(f)] = pre[h, side(f, s)]
+
+    def w_first(t):
+        return w1[t, 0:256]
+
+    def conv_first(f, ref):
+        lhs = cat(windows(ref) + windows(t27.at[f]))
+        rhs = cat([w_first(t) for t in range(TAPS)] + [we[a] for a in range(3)], 0)
+        split(pre, (face_rows(f),), dot(lhs, rhs))
+
+    def first_part(lo, hi):
+        @pl.loop(lo, hi)
+        def _(i):
+            for u in range(2):
+                fill(xc[u], xv[2 * i + u])
+            for u in range(2):
+                conv_first(2 * i + u, xc[u])
+
+    first_part(0, 3)
+    first.middle()
+    first_part(3, 6)
+    cload.wait()
+
+    @pl.loop(0, faces)
+    def _(f):
+        for h in range(2):
+            ff[h] = cv[f, :, 128 * h : 128 * h + 128].astype(f32)
+            for s in range(2):
+                cvf[h, s, ring_v(f)] = ff[h, pl.ds(area - cols if s else 0, cols)]
+                chf[h, s, ring_h(f)] = ff[h, pl.ds(cols - 1 if s else 0, rows, stride=cols)]
+
+    for s in range(2):
+        cev[s] = join(cvf, (s,)).astype(bf)
+        ceh[s] = join(chf, (s,)).astype(bf)
+    first.finish()
+    ring_in(first, 3)
+    ring_cat(rc1v, rc1h, 3)
+    for s in range(2):
+        rhs = cat([w_first(6 * s + b) for b in range(3)] + [we[2 * s]], 0)
+        split(cvf, (s,), dot(rc1v[s], rhs))
+        rhs = cat([w_first(3 * a + 2 * s) for a in range(3)] + [we[a] for a in range(3)], 0)
+        split(chf, (s,), dot(rc1h[s], rhs))
+    add_to_edges(cvf, chf)
+    for h in range(2):
+        for s in range(2):
+            evf[h, s], slev[h, s] = gelu_slope(evf[h, s])
+            ehf[h, s], sleh[h, s] = gelu_slope(ehf[h, s])
+    edges_out(second, 2)
+    second.start()
+
+    def conv_second(f):
+        lhs = cat(windows(hc.at[f]))
+        rhs = cat([w2[t] for t in range(TAPS)], 0)
+        split(pre, (face_rows(f),), dot(lhs, rhs))
+
+    def second_part(lo, hi):
+        @pl.loop(lo, hi)
+        def _(i):
+            for u in range(2):
+                f = 2 * i + u
+                act, sl = gelu_slope(join(pre, (face_rows(f),)))
+                slope[face_rows(f)] = sl.astype(bf)
+                fill(hc.at[f], act.astype(bf).reshape(rows, cols, 256))
+            for u in range(2):
+                conv_second(2 * i + u)
+
+    w2load.wait()
+    second_part(0, 3)
+    second.middle()
+    second_part(3, 6)
+    second.finish()
+    ring_in(second, 2)
+    ring_cat(rc2v, rc2h, 2)
+    for s in range(2):
+        split(cvf, (s,), dot(rc2v[s], cat([w2[6 * s + b] for b in range(3)], 0)))
+        split(chf, (s,), dot(rc2h[s], cat([w2[3 * a + 2 * s] for a in range(3)], 0)))
+    add_to_edges(cvf, chf)
+
+    def ring_grads(ex, taps, blocks):
+        for s in range(2):
+            lhs = cat([cat([rvf[j, s, pl.ds(12 * b, 216)] for j in range(2)]).astype(bf) for b in range(3)])
+            base = 0 if s else 6
+            rhs = cat([taps(8 - (base + b)) for b in range(3)], 1)
+            out = dot_nt(lhs, rhs)
+            if blocks == 3:
+                mid = dot_nt(gev[s], we[2 * s])
+                pad = jnp.zeros((24, LANES), f32)
+                mid = cat([pad, mid, pad], 0)
+                tail = mid[24:240]
+                for b in (1, 2):
+                    tail = tail + pltpu.roll(mid[24 - 12 * b : 240 - 12 * b], LANES - 9 * b, axis=1)
+                out = cat([out, jnp.where(lane < 9, tail, 0.0)])
+            for j in range(blocks):
+                cvf[j, s] = out[12:204, 128 * j : 128 * j + 128]
+                ff[j, pl.ds(256 * s, 12)] = out[0:12, 128 * j : 128 * j + 128]
+                ff[j, pl.ds(256 * s + 128, 12)] = out[204:216, 128 * j : 128 * j + 128]
+            lhs = cat([cat([rhf[j, s, pl.ds(12 * a, 384)] for j in range(2)]).astype(bf) for a in range(3)])
+            base = 0 if s else 2
+            rhs = cat([taps(8 - (base + 3 * a)) for a in range(3)], 1)
+            out = dot_nt(lhs, rhs)
+            if blocks == 3:
+                tail = dot_nt(lhs, cat([we[2 - a] for a in range(3)], 1))
+                tail = pltpu.roll(tail, LANES - 18, axis=1) if s else tail
+                out = cat([out, jnp.where(lane < 9, tail, 0.0)])
+            for j in range(blocks):
+                chf[j, s] = out[:, 128 * j : 128 * j + 128]
+        for j in range(blocks):
+            lanes = slice(128 * j, 128 * j + 128)
+            for spot in range(4):
+                s, right = spot // 2, spot % 2
+                v = ff[j, pl.ds(256 * s + 128 * right, 12)]
+                edge = (tx == 3) if right else (tx == 0)
+                late = jnp.where(edge, ty == 1, right == 0)
+                zero = jnp.zeros((4, LANES), f32)
+                ex.rg_c[spot, :, lanes] = jnp.where(late, cat([zero, v], 0), cat([v, zero], 0)).astype(bf)
+
+                @pl.when((ty == s) & edge)
+                def _(j=j, s=s, right=right, spot=spot, v=v):
+                    take = rule[spot, 0:12] > 0.0
+                    cvf[j, s, pl.ds(180 if right else 0, 12)] += jnp.where(take, v, 0.0)
+                    chf[j, right, pl.ds(372 if s else 0, 12)] += jnp.where(take, 0.0, v)
+        for s in range(2):
+            ex.rg_v[s] = join(cvf, (s,), blocks).astype(bf)
+            ex.rg_h[s] = join(chf, (s,), blocks).astype(bf)
+
+    def edge_grads(make_v, make_h):
+        for s in range(2):
+            for h in range(2):
+                lanes = slice(128 * h, 128 * h + 128)
+                v = make_v(h, s).astype(bf)
+                gev[s, :, lanes] = v
+                rvf[h, s, pl.ds(0, 24)] = jnp.zeros((24, LANES), f32)
+                rvf[h, s, pl.ds(216, 24)] = jnp.zeros((24, LANES), f32)
+                rvf[h, s, pl.ds(24, 192)] = v.astype(f32)
+                v = make_h(h, s).astype(bf)
+                geh[s, :, lanes] = v
+                rhf[h, s, pl.ds(12, 384)] = v.astype(f32)
+
+    def slope_two(u, h):
+        return gelu_slope(u + biases[1:2, 128 * h : 128 * h + 128].astype(f32))[1]
+
+    edge_grads(
+        lambda h, s: slope_two(evf[h, s], h) * cev[s, :, 128 * h : 128 * h + 128].astype(f32),
+        lambda h, s: slope_two(ehf[h, s], h) * ceh[s, :, 128 * h : 128 * h + 128].astype(f32),
+    )
+    ring_grads(third, lambda t: w2[t], 2)
+    third.start()
+
+    def out_copy(u, f):
+        return pltpu.make_async_copy(ost.at[u], out_ref.at[f], lsem.at[3 + u])
+
+    def third_part(lo, hi):
+        @pl.loop(lo, hi)
+        def _(i):
+            grads = []
+            for u in range(2):
+                f = 2 * i + u
+                act, sl = gelu_slope(join(pre, (face_rows(f),)) + biases[1:2].astype(f32))
+                cot = cv[f]
+                grad = (cot.astype(f32) * sl).astype(bf)
+                accb[2432:2433] += jnp.sum(grad.astype(f32), axis=0, keepdims=True)
+                fill(xc[u], grad.reshape(rows, cols, 256))
+                field = cat([xv[f].reshape(area, 256), t27[f, 1 : rows + 1].reshape(area, LANES)])
+                skip = dot(field, cat([wskip[0:256], wse[...]], 0))
+                fresh = dot_tn(field, cot)
+                acca[2304:2560] += fresh[0:256]
+                accb[2400:2432] += fresh[256:288]
+
+                @pl.when(i > 0)
+                def _(u=u, f=f):
+                    out_copy(u, f).wait()
+
+                ost[u] = (act + skip).astype(bf)
+                out_copy(u, f).start()
+                grads.append(grad)
+            pair = cat(grads, 0)
+            for a in range(3):
+                field = cat([hc[2 * i + u, a : a + rows].reshape(area, 768) for u in range(2)], 0)
+                acca[768 * a : 768 * a + 768] += dot_tn(field, pair)
+            rhs = cat([w2[8 - t] for t in range(TAPS)], 1)
+            for u in range(2):
+                split(pre, (face_rows(2 * i + u),), dot_nt(cat(windows(xc[u])), rhs))
+
+    third_part(0, 3)
+    third.middle()
+    third_part(3, 6)
+    for u in range(2):
+        out_copy(u, 0).wait()
+
+    def ring_kernel_grads(grad_ref, extra, rcv, rch):
+        for s in range(2):
+            fresh = dot_tn(rcv[s], gev[s])
+            grad_ref[1536 * s : 1536 * s + 768] += fresh[0:768]
+            if extra:
+                grad_ref[2304 + 64 * s : 2336 + 64 * s] += fresh[768:800]
+            fresh = dot_tn(rch[s], geh[s])
+            for a in range(3):
+                t = 3 * a + 2 * s
+                grad_ref[256 * t : 256 * t + 256] += fresh[256 * a : 256 * a + 256]
+                if extra:
+                    grad_ref[2304 + 32 * a : 2336 + 32 * a] += fresh[768 + 128 * a : 800 + 128 * a]
+
+    ring_kernel_grads(acca, False, rc2v, rc2h)
+    total_a = Total(0, acca, outa, 0, landa, 0)
+    total_b = Total(1, accb, slope, 3584, slope, 0)
+    total_a.to_core()
+    third.finish()
+    third.stage(2)
+
+    @pl.loop(0, faces)
+    def _(f):
+        for h in range(2):
+            for s in range(2):
+                pre[h, top(f, s)] += evf[h, s, ring_v(f)]
+        for h in range(2):
+            for s in range(2):
+                pre[h, side(f, s)] += ehf[h, s, ring_h(f)]
+        for h in range(2):
+            for s in range(2):
+                evf[h, s, ring_v(f)] = pre[h, top(f, s)]
+                ehf[h, s, ring_h(f)] = pre[h, side(f, s)]
+
+    edge_grads(lambda h, s: evf[h, s] * slev[h, s], lambda h, s: ehf[h, s] * sleh[h, s])
+    ring_grads(fourth, w_first, 3)
+    fourth.start()
+    total_a.to_x()
+
+    def fourth_part(lo, hi):
+        @pl.loop(lo, hi)
+        def _(i):
+            grads = []
+            for u in range(2):
+                f = 2 * i + u
+                grad = (join(pre, (face_rows(f),)) * slope[face_rows(f)].astype(f32)).astype(bf)
+                fill(hc.at[f], grad.reshape(rows, cols, 256))
+                fill(xc[u], xv[f])
+                grads.append(grad)
+            pair = cat(grads, 0)
+            for a in range(3):
+                field = cat([xc[u][a : a + rows].reshape(area, 768) for u in range(2)], 0)
+                accb[768 * a : 768 * a + 768] += dot_tn(field, pair)
+                extra = cat([t27[2 * i + u, a : a + rows].reshape(area, LANES) for u in range(2)], 0)
+                accb[2304 + 32 * a : 2336 + 32 * a] += dot_tn(extra, pair)[0:32]
+
+    fourth_part(0, 3)
+    fourth.middle()
+    total_a.to_group()
+    fourth_part(3, 6)
+    for q in range(8):
+        @pl.when(place != q)
+        def _(q=q):
+            pl.semaphore_signal(credit.at[2], inc=1, device_id=dev(q // 4, q % 4), device_id_type=pl.DeviceIdType.MESH)
+    for c, mate in ((0, core_mate), (1, x_mate)):
+        pl.semaphore_signal(credit.at[c], inc=1, device_id={"dp": mate}, device_id_type=pl.DeviceIdType.MESH)
+    ring_kernel_grads(accb, True, rc1v, rc1h)
+    total_b.to_core()
+    total_a.from_group()
+    fourth.finish()
+    fourth.stage(3)
+
+    def gx_copy(f):
+        return pltpu.make_async_copy(ost.at[f % 2], gx_ref.at[f], lsem.at[3 + f % 2])
+
+    def last_face(f):
+        cot = cv[f]
+        lhs = cat(windows(hc.at[f]) + [cot])
+        rhs = cat([w_first(8 - t) for t in range(TAPS)] + [wskip[0:256]], 1)
+        main = dot_nt(lhs, rhs)
+        for h in range(2):
+            ff[h] = main[:, 128 * h : 128 * h + 128]
+        lhs = cat([hc[f, a : a + rows, :, 256:512].reshape(area, 256) for a in range(3)] + [cot])
+        packed = dot_nt(lhs, cat([we[2], we[1], we[0], wse[...]], 1))
+        col = lax.broadcasted_iota(jnp.int32, (area, 1), 0) % cols
+        after = jnp.where(col == cols - 1, 0.0, pltpu.roll(packed, area - 1, axis=0))
+        before = jnp.where(col == 0, 0.0, pltpu.roll(packed, 1, axis=0))
+        ff[2] = after + pltpu.roll(packed, LANES - 9, axis=1) + pltpu.roll(before, LANES - 18, axis=1)
+        for j in range(3):
+            for s in range(2):
+                ff[j, pl.ds(area - cols if s else 0, cols)] += evf[j, s, ring_v(f)]
+        for j in range(3):
+            for s in range(2):
+                ff[j, pl.ds(cols - 1 if s else 0, rows, stride=cols)] += ehf[j, s, ring_h(f)]
+        for c in range(cols):
+            here = ff[2, pl.ds(c, rows, stride=cols)].astype(bf)
+            rc1h[c // 8, rows16(f * rows, rows), c % 8 * LANES : c % 8 * LANES + LANES] = here
+
+        @pl.when(f > 1)
+        def _():
+            gx_copy(f).wait()
+
+        ost[f % 2] = cat([ff[0], ff[1]]).astype(bf)
+        gx_copy(f).start()
+
+    def last_part(lo, hi):
+        @pl.loop(lo, hi)
+        def _(f):
+            last_face(f)
+
+    last_part(0, 4)
+    total_b.to_x()
+    total_a.back_x()
+    last_part(4, 8)
+    total_b.to_group()
+    total_a.back_core()
+    last_part(8, 12)
+    total_b.from_group()
+    total_a.finish(suma_ref, 8)
+    hot = packing([(0, 0)])
+    back = dot_nt(rc1h[0, :, 0 : span // 2], hot[:, 0 : span // 2]) + dot_nt(rc1h[1, :, 0 : span // 2], hot[:, span // 2 :])
+    for f in range(faces):
+        ev[f] = back[f * rows : f * rows + rows].T.astype(bf).reshape(9, cols, rows)
+    eout = pltpu.make_async_copy(ev, gext_ref, lsem.at[1])
+    eout.start()
+    total_b.back_x()
+    for u in range(2):
+        gx_copy(u).wait()
+    total_b.back_core()
+    total_b.finish(sumb_ref, 9)
+    eout.wait()
+    total_a.store.wait()
+    total_b.store.wait()
+    for ex in (first, second, third, fourth):
+        ex.drain()
+
+
+def fast_device(
+    features, extra_inputs, first_kernel, first_bias, second_kernel, second_bias,
+    skip_kernel, skip_bias, seam_table, cotangent,
+):
+    f32, bf = jnp.float32, jnp.bfloat16
+    _, faces, rows, cols, ch = features.shape
+    area = rows * cols
+    extra = extra_inputs.shape[-1]
+    biases = jnp.stack([first_bias, second_bias, skip_bias])
+    vm, hbm = pl.BlockSpec(memory_space=pltpu.VMEM), pl.BlockSpec(memory_space=pl.ANY)
+    shape = jax.ShapeDtypeStruct
+
+    def exchange_bufs(lanes, windows):
+        return [
+            pltpu.VMEM((2, 192, lanes), bf), pltpu.VMEM((2, 384, lanes), bf), pltpu.VMEM((384, lanes), bf),
+            pltpu.VMEM((384, lanes), bf), pltpu.VMEM((2, 192, lanes), bf), pltpu.VMEM((2, 384, lanes), bf),
+            pltpu.VMEM((4, 16, lanes), bf), pltpu.VMEM((8 * windows, 16, lanes), bf),
+            pltpu.VMEM((2 * windows, 16, lanes), bf),
+        ]
+
+    cat_shape = (rows + 2, cols, 3 * ch)
+    sums = (SUM_ROWS, ch)
+    scratch = [
+        pltpu.VMEM((TAPS, ch + extra, ch), bf), pltpu.VMEM((TAPS, ch, ch), bf), pltpu.VMEM((ch + extra, ch), bf),
+        pltpu.VMEM((3, LANES, ch), bf), pltpu.VMEM((LANES, ch), bf), pltpu.VMEM((384, 384), bf),
+        pltpu.VMEM((4, 16, LANES), f32),
+        pltpu.VMEM((faces, rows, cols, ch), bf), pltpu.VMEM((faces, extra, cols, rows), bf),
+        pltpu.VMEM((faces, area, ch), bf), pltpu.VMEM((faces, rows + 2, cols, LANES), bf),
+        [pltpu.VMEM(cat_shape, bf)] * 2, pltpu.VMEM((faces,) + cat_shape, bf),
+        pltpu.VMEM((2, faces * area, LANES), f32), pltpu.VMEM((faces * area, ch), bf),
+        pltpu.VMEM((2, 2, 192, LANES), f32), pltpu.VMEM((2, 2, 384, LANES), f32),
+        pltpu.VMEM((2, 192, ch), bf), pltpu.VMEM((2, 384, ch), bf),
+        pltpu.VMEM((2, area, ch), bf),
+        pltpu.VMEM((3, area, LANES), f32),
+        pltpu.VMEM((3, 2, 192, LANES), f32), pltpu.VMEM((3, 2, 384, LANES), f32),
+        pltpu.VMEM((3, 2, 240, LANES), f32), pltpu.VMEM((3, 2, 408, LANES), f32),
+        pltpu.VMEM((3, 2, 192, LANES), f32), pltpu.VMEM((3, 2, 384, LANES), f32),
+        pltpu.VMEM((2, 192, 896), bf), pltpu.VMEM((2, 384, 1152), bf),
+        pltpu.VMEM((2, 192, 768), bf), pltpu.VMEM((2, 384, 768), bf),
+        pltpu.VMEM((2, 192, ch), bf), pltpu.VMEM((2, 384, ch), bf),
+        pltpu.VMEM(sums, f32), pltpu.VMEM(sums, f32), pltpu.VMEM(sums, bf), pltpu.VMEM(sums, bf),
+        [exchange_bufs(384, 0 + 1), exchange_bufs(256, 1), exchange_bufs(256, 1), exchange_bufs(384, 1)],
+        pltpu.SemaphoreType.DMA((4, 48)), pltpu.SemaphoreType.DMA((4, 33)),
+        pltpu.SemaphoreType.DMA((2, 20)), pltpu.SemaphoreType.DMA((2, 20)),
+        pltpu.SemaphoreType.REGULAR((3,)), pltpu.SemaphoreType.REGULAR((2, 2)), pltpu.SemaphoreType.DMA((10,)),
+    ]
+    out = pl.pallas_call(
+        whole_block,
+        out_shape=(
+            shape((faces, area, ch), bf), shape((faces, area, ch), bf), shape((faces, extra, cols, rows), bf),
+            shape(sums, bf), shape(sums, bf),
+        ),
+        in_specs=[hbm] * 5 + [vm] * 2 + [hbm],
+        out_specs=[hbm] * 5,
+        scratch_shapes=scratch,
+        compiler_params=pltpu.CompilerParams(
+            collective_id=0, has_side_effects=True, vmem_limit_bytes=65400 * 1024),
+    )(
+        features[0], extra_inputs[0].transpose(0, 3, 2, 1), first_kernel.reshape(TAPS, ch + extra, ch),
+        second_kernel.reshape(TAPS, ch, ch), skip_kernel, biases, seam_table.transpose(1, 2, 0),
+        cotangent.reshape(faces, area, ch),
+    )
+    block_output, grad_features, grad_extra, second_sum, first_sum = out
+    tall = TAPS * ch
+    tail = first_sum[tall : tall + 96].reshape(3, 32, ch)
+    first_grad = jnp.concatenate(
+        [first_sum[:tall].reshape(3, 3, ch, ch), tail[:, :PACK].reshape(3, 3, extra, ch)], 2)
+    skip = first_sum[tall + 96 : tall + 128]
+    return (
+        block_output.reshape(features.shape),
+        grad_features.reshape(features.shape),
+        grad_extra.transpose(0, 3, 2, 1)[None],
+        first_grad.astype(f32),
+        tail[1, ONE].astype(f32),
+        second_sum[:tall].reshape(3, 3, ch, ch).astype(f32),
+        first_sum[tall + 128].astype(f32),
+        jnp.concatenate([second_sum[tall:], skip[extra : 2 * extra]], 0).astype(f32),
+        skip[ONE].astype(f32),
+    )
+
+
 def solution(mesh):
+    fits = mesh.shape["ty"] == 2 and mesh.shape["tx"] == 4
+
+    def block(*args):
+        tile = args[0].shape
+        if fits and tile[1:] == (12, 32, 16, 256) and args[1].shape[-1] == 9:
+            return fast_device(*args)
+        return per_device(*args)
+
     return jax.shard_map(
-        per_device,
+        block,
         mesh=mesh,
         in_specs=(
             P("dp", None, "ty", "tx", None),

time: 1240 us -> 174 us (0.14)
  waiting for transfers between devices: 459 us -> 0 us
  matrix products: 389 us -> 0 us
  Pallas kernels: 0 us -> 155 us
  other arithmetic: 159 us -> 6.55 us
  local copies, waits for them, and re-layouts: 125 us -> 11.5 us
  starting transfers between devices: 49.4 us -> 0 us
  blocking collectives: 42.4 us -> 0 us
  between operations: 16.5 us -> 0.7 us
    psum x3 -> x0, waiting for transfers between devices: 296 us -> none  [the longest x2 163 us: collect(): edge_grads = lax.psum(edge_grads, ('ty', 'tx'))]
    conv_general_dilated x4 -> x0, matrix products: 294 us -> none  [conv_valid(): lax.conv_general_dilated(merged, kernel, (1, 1), 'VALID', dimension_numbe...]
    pallas_call x0 -> x1, Pallas kernels: none -> 155 us  [fast_device(): pl.pallas_call(whole_block, out_shape=(shape((faces, area, ch), bf), shap...]
    all_gather x4 -> x0, waiting for transfers between devices: 149 us -> none  [the longest x2 135 us: face_edges(): lax.all_gather(column_edges[None], ('ty', 'tx'), axis=0, tiled=True)]
    dot_general x25 -> x0, matrix products: 94.6 us -> none  [the longest x18 60.2 us: kernel_grad(): jnp.einsum('sfhwc,sfhwd->cd', window, grad_pre, preferred_element_type=jn...]
    ppermute x16 -> x0, starting transfers between devices: 48.5 us -> none  [the longest x8 37.7 us: extended(): before = lax.ppermute(last, axis, up)]
    psum x1 -> x0, blocking collectives: 42.4 us -> none  [per_device(): lax.psum((first_kernel_grad, first_bias_grad, second_kernel_grad, second_...]
    scatter-add x24 -> x0, other arithmetic: 38.1 us -> none  [the longest x2 6.4 us: collect(): inside = inside.at[:, :, 0, -1].add(widened[:, :, 0, tile_columns + 3])]
  transfers between devices with their start and end apart: 23 -> 0, of which waited for: 10 -> 0; matrix products, arithmetic and copies ran while one was open for 20% -> 0% of each run, Pallas kernels for 0% -> 0%
where the time goes in v1:
time: 174 us
  Pallas kernels  155 us (89%)
  local copies, waits for them, and re-layouts  11.5 us (7%)
  other arithmetic  6.55 us (4%)
    pallas_call x1, Pallas kernels, fast_device(): pl.pallas_call(whole_block, out_shape=(shape((faces, area, ch), bf), shap...  155 us
    unnamed x11, local copies, waits for them, and re-layouts  6.57 us

profile of v1, /device:TPU:0, one launch (start us, length us, event | category | flops | bytes accessed | tf_op | source)
XLA Modules:
  0.0 173.6 jit_solution(8663410454840681282)
XLA Ops:
  0.6 0.7 stack.12
  1.3 0.7 stack.13
  2.0 0.7 stack.14
  2.6 0.6 pad_maximum_fusion.biases
  3.2 154.8 %shard_map.169 = (bf16[12,512,256]{2,1,0:T(8,128)(2,1)}, bf16[12,512,256]{2,1,0:T(8,128)(2,1)}, bf16[12,9,16,32]{3,2,1,0:T(8,128)(2,1)}, bf16[2560,256]{1,0:T(8,128)(2,1)}, bf16[2560,256]{1,0:T(8,128)(2,1)}) custom-call(bf16[12,32,16,256]{3,2,1,0:T(8,128)(2,1)} %bitcast.25, bf16[12,9,16,32]{3,2,1,0:T(8,128)(2,1)} %bitcast.30, bf16[9,265,256]{2,1,0:T(8,128)(2,1)} %bitcast.27, ...), custom_call_target="tpu_custom_call" | custom-call | tf_op jit(solution)/shard_map/pallas_call | solution.py:1271
  158.0 0.0 copy-start.2
  158.1 1.4 slice_convert_fusion.1
  159.4 0.7 slice.37
  160.1 0.8 slice.31
  160.9 1.3 slice.30
  162.3 0.6 slice_convert_fusion
  162.9 0.0 copy-done.2
  162.9 0.1 slice.34
  163.0 0.7 maximum_convert_fusion.1
  163.7 1.6 convert.4
  165.3 0.0 copy-start.1
  165.3 1.7 maximum_convert_fusion
  167.0 1.1 copy-done.1
  168.1 0.0 copy-start
  168.1 1.7 copy.22
  169.8 1.4 copy-done
  171.2 1.7 copy.23
  172.8 0.0 copy-done.3
  172.8 0.8 copy.24
  (3 shorter events, 0.0 us)
Async XLA Ops:
  158.0 4.8 %copy-start.2 = (bf16[2560,256]{1,0:T(8,128)(2,1)S(1)}, bf16[2560,256]{1,0:T(8,128)(2,1)}, u32[]{:S(2)}) copy-start(bf16[2560,256]{1,0:T(8,128)(2,1)} %get-tuple-element.18) | copy-start | bytes 3932164
  165.3 2.8 %copy-start.1 = (bf16[12,512,256]{2,1,0:T(8,128)(2,1)S(1)}, bf16[12,512,256]{2,1,0:T(8,128)(2,1)}, u32[]{:S(2)}) copy-start(bf16[12,512,256]{2,1,0:T(8,128)(2,1)} %get-tuple-element.14) | copy-start | bytes 9437188
  168.1 3.0 %copy-start = (bf16[12,512,256]{2,1,0:T(8,128)(2,1)S(1)}, bf16[12,512,256]{2,1,0:T(8,128)(2,1)}, u32[]{:S(2)}) copy-start(bf16[12,512,256]{2,1,0:T(8,128)(2,1)} %get-tuple-element.15) | copy-start | bytes 9437188
  171.2 1.7 copy-start.3

commit v2 on v1

--- a/solution.py
+++ b/solution.py
@@ -2,6 +2,8 @@
 
 import jax
 import jax.numpy as jnp
+import ml_dtypes
+import numpy as np
 from jax import lax
 from jax.experimental import pallas as pl
 from jax.experimental.pallas import tpu as pltpu
@@ -289,12 +291,32 @@
 LANES = 128
 PACK = 27
 ONE = 27
+FOUR = ("core", "x", "y", "z")
+THREE = ("core", "x", "yz")
+SUMS = (("a", 0, 2560, FOUR), ("b", 0, 1024, THREE), ("c", 1024, 512, THREE), ("d", 1536, 512, THREE), ("e", 2048, 512, THREE))
+BLOCKS = (0, 1024, 1792)
+SUM_PLAN = {
+    ("middle", 0): (("a", 0),),
+    ("back", 2): (("a", 1),),
+    ("sent", 0): (("a", 2),),
+    ("first", 0): (("b", 0), ("a", 3)),
+    ("more", 4): (("c", 0), ("b", 1)),
+    ("more", 6): (("a", 4),),
+    ("third", 0): (("d", 0), ("e", 0), ("c", 1)),
+    ("last", 1): (("d", 1), ("e", 1), ("b", 2), ("a", 5)),
+    ("last", 2): (("c", 2),),
+    ("last", 3): (("d", 2), ("e", 2), ("b", 3), ("a", 6)),
+    ("last", 4): (("c", 3),),
+    ("last", 5): (("d", 3), ("e", 3), ("b", 4)),
+    ("end", 0): (("c", 4), ("a", 7), ("d", 4), ("e", 4), ("b", 5)),
+    ("rest", 0): (("c", 5), ("d", 5), ("e", 5), ("a", 8), ("b", 6), ("c", 6), ("d", 6), ("e", 6)),
+}
 
 
 def whole_block(
-    x_in, ext_in, w1_in, w2_in, skip_in, biases, table, cot_in,
-    out_ref, gx_ref, gext_ref, suma_ref, sumb_ref,
-    w1, w2, wskip, we, wse, sel_t, rule,
+    x_in, ext_in, w1_in, w2_in, skip_in, bias_one, bias_two, bias_skip, table, cot_in, hot_in, hot_back_in,
+    out_ref, gx_ref, gext_ref, suma_ref, sumb_ref, tails, rests,
+    w1, w2, wskip, we, wse, we81, sel_t, rule,
     xv, ev, cv, t27, xc, hc, pre, slope, slev, sleh, cev, ceh,
     ost, ff, evf, ehf, rvf, rhf, cvf, chf, rc1v, rc1h, rc2v, rc2h, gev, geh,
     acca, accb, outa, landa, bufs, ssem, rsem, sum_ssem, sum_rsem, credit, ack, lsem,
@@ -328,41 +350,47 @@
     def flip48(flag, k, n):
         return 48 * jnp.where(flag, n - 1 - k, k)
 
+    def maybe(cond, call):
+        if cond is None:
+            call()
+        else:
+            pl.when(cond)(call)
+
     class Exchange:
         def __init__(self, index):
             self.index = index
             self.ed_v, self.ed_h, self.db, self.sb, self.rg_v, self.rg_h, self.rg_c, self.xw, self.xd = bufs[index]
-            self.sent = []
-            self.slot = 0
-
-        def send(self, cond, src, dst, rs, target):
-            copy = pltpu.make_async_remote_copy(
-                src_ref=src, dst_ref=dst, send_sem=ssem.at[self.index, self.slot],
-                recv_sem=rsem.at[self.index, rs], device_id=target, device_id_type=pl.DeviceIdType.MESH,
-            )
-            self.slot += 1
-            self.sent.append((cond, copy))
-            if cond is None:
-                copy.start()
-            else:
-                pl.when(cond)(copy.start)
+
+        def copies(self, sends, first_slot):
+            for n, (cond, src, dst, rs, target) in enumerate(sends):
+                yield cond, pltpu.make_async_remote_copy(
+                    src_ref=src, dst_ref=dst, send_sem=ssem.at[self.index, first_slot + n],
+                    recv_sem=rsem.at[self.index, rs], device_id=target, device_id_type=pl.DeviceIdType.MESH,
+                )
+
+        def start(self):
+            for cond, copy in self.copies(self.first_sends(), 0):
+                maybe(cond, copy.start)
+            self.first_moves()
+
+        def middle(self):
+            self.relay()
+            for cond, copy in self.copies(self.second_sends(), 24):
+                maybe(cond, copy.start)
+            self.second_moves()
+
+        def drain(self):
+            for cond, copy in self.copies(self.first_sends(), 0):
+                maybe(cond, copy.wait_send)
+            for cond, copy in self.copies(self.second_sends(), 24):
+                maybe(cond, copy.wait_send)
 
         def get(self, cond, dst, rs):
             copy = pltpu.make_async_remote_copy(
                 src_ref=dst, dst_ref=dst, send_sem=ssem.at[self.index, 0],
                 recv_sem=rsem.at[self.index, rs], device_id=dev(1 - ty, tx), device_id_type=pl.DeviceIdType.MESH,
             )
-            if cond is None:
-                copy.wait_recv()
-            else:
-                pl.when(cond)(copy.wait_recv)
-
-        def drain(self):
-            for cond, copy in self.sent:
-                if cond is None:
-                    copy.wait_send()
-                else:
-                    pl.when(cond)(copy.wait_send)
+            maybe(cond, copy.wait_recv)
 
         def move(self, cond, dst, dst_at, src, src_at):
             @pl.when(cond)
@@ -370,29 +398,35 @@
                 dst[dst_at] = src[src_at]
 
     class Forward(Exchange):
-        def start(self):
-            ed_v, ed_h, db = self.ed_v, self.ed_h, self.db
+        def row_pieces(self):
+            to = rows16((2 * ty) * 96 + hx * 48, 48)
             for k in range(4):
-                at = rows16(flip48(hx == 1, k, 4), 48)
-                to = rows16((2 * ty) * 96 + hx * 48, 48)
-                y, x = home_class(k)
-                self.send(kk != k, ed_v.at[ty, at], db.at[to], (2 * ty) * 2 + hx, dev(y, x))
-                self.move(kk == k, db, (to,), ed_v, (ty, at))
+                yield k, rows16(flip48(hx == 1, k, 4), 48), to
+
+        def column_pieces(self):
+            to = rows16(jnp.where(hx == 1, 1, 3) * 96 + ty * 48, 48)
             for m in range(8):
-                at = rows16(flip48(ty == 1, m, 8), 48)
-                side = jnp.where(hx == 1, 1, 3)
-                to = rows16(side * 96 + ty * 48, 48)
-                y, x = home(m)
-                self.send(at_end & (mm != m), ed_h.at[hx, at], db.at[to], side * 2 + ty, dev(y, x))
-                self.move(at_end & (mm == m), db, (to,), ed_h, (hx, at))
-            rg_v, rg_h, rg_c = self.rg_v, self.rg_h, self.rg_c
-            self.send(None, ed_v.at[1 - ty], rg_v.at[ty], 24, dev(1 - ty, tx))
-            self.send(tx < 3, ed_h.at[1], rg_h.at[0], 25, dev(ty, tx + 1))
-            self.send(tx > 0, ed_h.at[0], rg_h.at[1], 26, dev(ty, tx - 1))
-            self.send(tx < 3, ed_v.at[1 - ty, pl.ds(176, 16)], rg_c.at[2 * ty], 20 + 2 * ty, dev(1 - ty, tx + 1))
-            self.send(tx > 0, ed_v.at[1 - ty, pl.ds(0, 16)], rg_c.at[2 * ty + 1], 21 + 2 * ty, dev(1 - ty, tx - 1))
-
-        def middle(self):
+                yield m, rows16(flip48(ty == 1, m, 8), 48), to
+
+        def first_sends(self):
+            ed_v, ed_h, db, rg_v, rg_h, rg_c = self.ed_v, self.ed_h, self.db, self.rg_v, self.rg_h, self.rg_c
+            for k, at, to in self.row_pieces():
+                yield kk != k, ed_v.at[ty, at], db.at[to], (2 * ty) * 2 + hx, dev(*home_class(k))
+            for m, at, to in self.column_pieces():
+                yield at_end & (mm != m), ed_h.at[hx, at], db.at[to], jnp.where(hx == 1, 2, 6) + ty, dev(*home(m))
+            yield None, ed_v.at[1 - ty], rg_v.at[ty], 24, dev(1 - ty, tx)
+            yield tx < 3, ed_h.at[1], rg_h.at[0], 25, dev(ty, tx + 1)
+            yield tx > 0, ed_h.at[0], rg_h.at[1], 26, dev(ty, tx - 1)
+            yield tx < 3, ed_v.at[1 - ty, pl.ds(176, 16)], rg_c.at[2 * ty], 20 + 2 * ty, dev(1 - ty, tx + 1)
+            yield tx > 0, ed_v.at[1 - ty, pl.ds(0, 16)], rg_c.at[2 * ty + 1], 21 + 2 * ty, dev(1 - ty, tx - 1)
+
+        def first_moves(self):
+            for k, at, to in self.row_pieces():
+                self.move(kk == k, self.db, (to,), self.ed_v, (ty, at))
+            for m, at, to in self.column_pieces():
+                self.move(at_end & (mm == m), self.db, (to,), self.ed_h, (hx, at))
+
+        def relay(self):
             db, sb = self.db, self.sb
             for t in range(4):
                 for h in range(2):
@@ -402,33 +436,46 @@
                         own = at_end & (ty == h) & (tx == (0 if t == 3 else 3))
                     self.get(jnp.logical_not(own), db.at[pl.ds(t * 96 + h * 48, 48)], t * 2 + h)
             sb[...] = dot_tn(sel_t[...], db[...]).astype(bf)
+
+        def out_rows(self):
             for y in range(2):
                 for h in range(2):
                     x = jnp.where(at_end, 3 * h, 1 + h)
                     own = (ty == y) & (tx == x)
-                    at = pl.ds(2 * y * 96 + h * 48, 48)
-                    to = rows16(48 * ((3 - kk) if h else kk), 48)
-                    self.send(jnp.logical_not(own), sb.at[at], self.rg_v.at[y, to], 8 + kk, dev(y, x))
-                    self.move(own, self.rg_v, (y, to), sb, (at,))
+                    yield own, y, x, pl.ds(2 * y * 96 + h * 48, 48), rows16(48 * ((3 - kk) if h else kk), 48)
+
+        def out_columns(self):
             for y in range(2):
                 for h in range(2):
                     own = (ty == y) & (tx == 3 * h)
                     at = pl.ds((1 if h else 3) * 96 + y * 48, 48)
-                    to = rows16(48 * ((7 - mm) if y else mm), 48)
-                    self.send(jnp.logical_not(own), sb.at[at], self.rg_h.at[h, to], 12 + mm, dev(y, 3 * h))
-                    self.move(own, self.rg_h, (h, to), sb, (at,))
+                    yield own, y, h, at, rows16(48 * ((7 - mm) if y else mm), 48)
+
+        def out_corners(self):
             for y in range(2):
                 for m, x, right, at in ((3, 1, 0, 32), (3, 2, 1, 48), (4, 3, 0, 80), (4, 0, 1, 0), (7, 2, 0, 32), (7, 1, 1, 48)):
-                    spot = 2 * y + right
-                    src = (pl.ds(2 * y * 96 + at, 16),)
-                    if home(m) == (y, x):
-                        self.move(mm == m, self.rg_c, (spot,), sb, src)
-                    else:
-                        self.send(mm == m, sb.at[src], self.rg_c.at[spot], 20 + spot, dev(y, x))
+                    yield m, y, x, 2 * y + right, pl.ds(2 * y * 96 + at, 16)
                 for h in range(2):
-                    spot = 2 * (1 - y) + h
-                    src = pl.ds((1 if h else 3) * 96 + (32 if y else 48), 16)
-                    self.send(mm == 7, sb.at[src], self.rg_c.at[spot], 20 + spot, dev(y, 3 * h))
+                    yield 7, y, 3 * h, 2 * (1 - y) + h, pl.ds((1 if h else 3) * 96 + (32 if y else 48), 16)
+
+        def second_sends(self):
+            sb = self.sb
+            for own, y, x, at, to in self.out_rows():
+                yield jnp.logical_not(own), sb.at[at], self.rg_v.at[y, to], 8 + kk, dev(y, x)
+            for own, y, h, at, to in self.out_columns():
+                yield jnp.logical_not(own), sb.at[at], self.rg_h.at[h, to], 12 + mm, dev(y, 3 * h)
+            for m, y, x, spot, at in self.out_corners():
+                if home(m) != (y, x):
+                    yield mm == m, sb.at[at], self.rg_c.at[spot], 20 + spot, dev(y, x)
+
+        def second_moves(self):
+            for own, y, x, at, to in self.out_rows():
+                self.move(own, self.rg_v, (y, to), self.sb, (at,))
+            for own, y, h, at, to in self.out_columns():
+                self.move(own, self.rg_h, (h, to), self.sb, (at,))
+            for m, y, x, spot, at in self.out_corners():
+                if home(m) == (y, x):
+                    self.move(mm == m, self.rg_c, (spot,), self.sb, (at,))
 
         def finish(self):
             self.get(None, self.rg_v.at[1 - ty], 24)
@@ -449,42 +496,45 @@
                 self.get(jnp.logical_not(skip), self.rg_c.at[spot], 20 + spot)
 
     class Backward(Exchange):
-        def start(self):
-            rg_v, rg_h, rg_c, sb, xw, xd = self.rg_v, self.rg_h, self.rg_c, self.sb, self.xw, self.xd
-            for k in range(4):
-                at = rows16(flip48(hx == 1, k, 4), 48)
-                to = rows16((2 * ty) * 96 + hx * 48, 48)
-                y, x = home_class(k)
-                self.send(kk != k, rg_v.at[ty, at], sb.at[to], (2 * ty) * 2 + hx, dev(y, x))
-                self.move(kk == k, sb, (to,), rg_v, (ty, at))
-            for m in range(8):
-                at = rows16(flip48(ty == 1, m, 8), 48)
-                side = jnp.where(hx == 1, 1, 3)
-                to = rows16(side * 96 + ty * 48, 48)
-                y, x = home(m)
-                self.send(at_end & (mm != m), rg_h.at[hx, at], sb.at[to], side * 2 + ty, dev(y, x))
-                self.move(at_end & (mm == m), sb, (to,), rg_h, (hx, at))
+        row_pieces, column_pieces = Forward.row_pieces, Forward.column_pieces
+        out_rows, out_columns = Forward.out_rows, Forward.out_columns
+
+        def corners(self):
             for right in range(2):
-                spot = 2 * ty + right
                 away = (tx < 3) if right else (tx > 0)
                 if right:
                     x, y = jnp.where(tx == 0, 1, jnp.where(tx == 1, 2, 3)), jnp.where(tx == 0, 0, 1)
                 else:
                     x, y = jnp.where(tx == 1, 3, jnp.where(tx == 2, 2, 1)), jnp.where(tx == 3, 0, 1)
                 own = away & (ty == y) & (tx == x)
-                slot = ty * 2 + right
-                self.send(away & jnp.logical_not(own), rg_c.at[spot], xw.at[slot], 8 + slot, dev(y, x))
-                self.move(own, xw, (slot,), rg_c, (spot,))
+                yield right, away, own, x, y, 2 * ty + right
+
+        def first_sends(self):
+            rg_v, rg_h, rg_c, sb, xw, xd = self.rg_v, self.rg_h, self.rg_c, self.sb, self.xw, self.xd
+            for k, at, to in self.row_pieces():
+                yield kk != k, rg_v.at[ty, at], sb.at[to], (2 * ty) * 2 + hx, dev(*home_class(k))
+            for m, at, to in self.column_pieces():
+                yield at_end & (mm != m), rg_h.at[hx, at], sb.at[to], jnp.where(hx == 1, 2, 6) + ty, dev(*home(m))
+            for right, away, own, x, y, slot in self.corners():
+                yield away & jnp.logical_not(own), rg_c.at[slot], xw.at[slot], 8 + slot, dev(y, x)
                 inner = 2 * (1 - ty) + right
                 edge = (tx == 3) if right else (tx == 0)
-                self.send(edge, rg_c.at[inner], xw.at[4 + ty * 2 + right], 12 + ty * 2 + right, dev(1, 2))
-                self.send(away, rg_c.at[inner], xd.at[1 - right], 16 + 1 - right, dev(1 - ty, tx + (1 if right else -1)))
+                yield edge, rg_c.at[inner], xw.at[4 + slot], 12 + slot, dev(1, 2)
+                yield away, rg_c.at[inner], xd.at[1 - right], 17 - right, dev(1 - ty, tx + (1 if right else -1))
             ed_v, ed_h = self.ed_v, self.ed_h
-            self.send(None, rg_v.at[1 - ty], ed_v.at[ty], 30, dev(1 - ty, tx))
-            self.send(tx < 3, rg_h.at[1], ed_h.at[0], 31, dev(ty, tx + 1))
-            self.send(tx > 0, rg_h.at[0], ed_h.at[1], 32, dev(ty, tx - 1))
-
-        def middle(self):
+            yield None, rg_v.at[1 - ty], ed_v.at[ty], 30, dev(1 - ty, tx)
+            yield tx < 3, rg_h.at[1], ed_h.at[0], 31, dev(ty, tx + 1)
+            yield tx > 0, rg_h.at[0], ed_h.at[1], 32, dev(ty, tx - 1)
+
+        def first_moves(self):
+            for k, at, to in self.row_pieces():
+                self.move(kk == k, self.sb, (to,), self.rg_v, (ty, at))
+            for m, at, to in self.column_pieces():
+                self.move(at_end & (mm == m), self.sb, (to,), self.rg_h, (hx, at))
+            for right, away, own, x, y, slot in self.corners():
+                self.move(own, self.xw, (slot,), self.rg_c, (slot,))
+
+        def relay(self):
             sb, db, xw = self.sb, self.db, self.xw
             for s in range(4):
                 for h in range(2):
@@ -512,21 +562,18 @@
                         here = pl.ds(spot, 16)
                         sb[here] = (sb[here].astype(f32) + xw[slot].astype(f32)).astype(bf)
             db[...] = dot(sel_t[...], sb[...]).astype(bf)
-            for y in range(2):
-                for h in range(2):
-                    x = jnp.where(at_end, 3 * h, 1 + h)
-                    own = (ty == y) & (tx == x)
-                    at = pl.ds(2 * y * 96 + h * 48, 48)
-                    to = rows16(48 * ((3 - kk) if h else kk), 48)
-                    self.send(jnp.logical_not(own), db.at[at], self.ed_v.at[y, to], 18 + kk, dev(y, x))
-                    self.move(own, self.ed_v, (y, to), db, (at,))
-            for y in range(2):
-                for h in range(2):
-                    own = (ty == y) & (tx == 3 * h)
-                    at = pl.ds((1 if h else 3) * 96 + y * 48, 48)
-                    to = rows16(48 * ((7 - mm) if y else mm), 48)
-                    self.send(jnp.logical_not(own), db.at[at], self.ed_h.at[h, to], 22 + mm, dev(y, 3 * h))
-                    self.move(own, self.ed_h, (h, to), db, (at,))
+
+        def second_sends(self):
+            for own, y, x, at, to in self.out_rows():
+                yield jnp.logical_not(own), self.db.at[at], self.ed_v.at[y, to], 18 + kk, dev(y, x)
+            for own, y, h, at, to in self.out_columns():
+                yield jnp.logical_not(own), self.db.at[at], self.ed_h.at[h, to], 22 + mm, dev(y, 3 * h)
+
+        def second_moves(self):
+            for own, y, x, at, to in self.out_rows():
+                self.move(own, self.ed_v, (y, to), self.db, (at,))
+            for own, y, h, at, to in self.out_columns():
+                self.move(own, self.ed_h, (h, to), self.db, (at,))
 
         def finish(self):
             self.get(None, self.ed_v.at[1 - ty], 30)
@@ -555,131 +602,140 @@
                     evf[j, 1 - ty, pl.ds(176, 16)] += self.xd[1, :, lanes].astype(f32)
 
     class Total:
-        def __init__(self, index, acc, out, out0, land, land0):
+        def __init__(self, index, acc, acc0, out, out0, land, land0, count, order):
             self.index, self.acc, self.out, self.land = index, acc, out, land
-            self.out0, self.land0 = out0, land0
-            self.half = SUM_ROWS // 2 * core
-            self.other_half = SUM_ROWS // 2 * (1 - core)
-            self.quarter = self.half + SUM_ROWS // 4 * xx
-            self.other_quarter = self.half + SUM_ROWS // 4 * (1 - xx)
-            self.own = self.quarter + SUM_ROWS // 32 * place
-
-        def copy(self, slot, src, dst, rslot, target):
+            self.acc0, self.out0, self.land0, self.count = acc0, out0, land0, count
+            axes = {
+                "core": (2, core, lambda k: {"dp": core_mate}),
+                "x": (2, xx, lambda k: {"dp": x_mate}),
+                "y": (2, ty, lambda k: {"ty": 1 - ty}),
+                "z": (4, tx, lambda k: {"tx": k}),
+                "yz": (8, place, lambda k: {"ty": k // 4, "tx": k % 4}),
+            }
+            self.stages = []
+            start, size, land_at, sem = 0, count, 0, 0
+            for name in order:
+                n, me, target = axes[name]
+                chunk = size // n
+                self.stages.append((n, me, target, start, chunk, land_at, sem))
+                land_at += chunk * (1 if n == 2 else n)
+                sem += 1 if n == 2 else n
+                start, size = start + me * chunk, chunk
+            self.unit, self.sems, self.last = size, sem, len(order) - 1
+            self.near = []
+            for n, me, *_ in self.stages:
+                if n == 2:
+                    self.near.append([(1 - me, None, 0, 0)])
+                else:
+                    self.near.append([(k, me != k, k, me) for k in range(n)])
+
+        def at(self, base, start, size):
+            return rows16(base + start, size)
+
+        def copy(self, src, dst, slot, rslot, target):
             return pltpu.make_async_remote_copy(
                 src_ref=src, dst_ref=dst, send_sem=sum_ssem.at[self.index, slot],
                 recv_sem=sum_rsem.at[self.index, rslot], device_id=target, device_id_type=pl.DeviceIdType.MESH,
             )
 
-        def outs(self, start, size):
-            return self.out.at[rows16(self.out0 + start, size)]
-
-        def lands(self, start, size):
-            return self.land.at[rows16(self.land0 + start, size)]
+        def rs_copy(self, s, k, mine, theirs):
+            n, me, target, start, chunk, land_at, sem = self.stages[s]
+            return self.copy(
+                self.out.at[self.at(self.out0, start + k * chunk, chunk)],
+                self.land.at[self.at(self.land0, land_at + chunk * theirs, chunk)],
+                sem + mine, sem + theirs, target(k))
+
+        def send_rs(self, s):
+            n, me, target, start, chunk, land_at, sem = self.stages[s]
+            for k, cond, mine, theirs in self.near[s]:
+                def go(k=k, mine=mine, theirs=theirs):
+                    self.cast(start + k * chunk, chunk)
+                    self.rs_copy(s, k, mine, theirs).start()
+                maybe(cond, go)
+
+        def recv_rs(self, s):
+            n, me, target, start, chunk, land_at, sem = self.stages[s]
+            for k, cond, mine, theirs in self.near[s]:
+                def get(k=k, mine=mine):
+                    here = self.land.at[self.at(self.land0, land_at + chunk * mine, chunk)]
+                    self.copy(here, here, sem + mine, sem + mine, target(k)).wait_recv()
+
+                    @pl.loop(0, chunk // self.unit)
+                    def _(i):
+                        self.acc[self.at(self.acc0, start + me * chunk + i * self.unit, self.unit)] += self.land[
+                            self.at(self.land0, land_at + chunk * mine + i * self.unit, self.unit)].astype(f32)
+
+                maybe(cond, get)
+
+        def done_rs(self, s):
+            target = self.stages[s][2]
+            for k, cond, mine, theirs in self.near[s]:
+                def done(k=k, mine=mine, theirs=theirs):
+                    self.rs_copy(s, k, mine, theirs).wait_send()
+                    pl.semaphore_signal(
+                        ack.at[self.index, s], inc=1, device_id=target(k), device_id_type=pl.DeviceIdType.MESH)
+                maybe(cond, done)
+
+        def ag_copy(self, s, k, mine, theirs):
+            n, me, target, start, chunk, land_at, sem = self.stages[s]
+            here = self.out.at[self.at(self.out0, start + me * chunk, chunk)]
+            return self.copy(here, here, self.sems + sem + mine, self.sems + sem + theirs, target(k))
+
+        def send_ag(self, s):
+            pl.semaphore_wait(ack.at[self.index, s], self.stages[s][0] - 1)
+            for k, cond, mine, theirs in self.near[s]:
+                maybe(cond, lambda k=k, mine=mine, theirs=theirs: self.ag_copy(s, k, mine, theirs).start())
+
+        def recv_ag(self, s):
+            n, me, target, start, chunk, land_at, sem = self.stages[s]
+            for k, cond, mine, theirs in self.near[s]:
+                def get(k=k, mine=mine):
+                    here = self.out.at[self.at(self.out0, start + k * chunk, chunk)]
+                    slot = self.sems + sem + mine
+                    self.copy(here, here, slot, slot, target(k)).wait_recv()
+                maybe(cond, get)
 
         def cast(self, start, size):
-            step = SUM_ROWS // 32
-
-            @pl.loop(0, size // step)
+            @pl.loop(0, size // self.unit)
             def _(i):
-                at = start + i * step
-                self.out[rows16(self.out0 + at, step)] = self.acc[rows16(at, step)].astype(bf)
-
-        def add(self, start, size, land):
-            step = SUM_ROWS // 32
-
-            @pl.loop(0, size // step)
-            def _(i):
-                self.acc[rows16(start + i * step, step)] += self.land[
-                    rows16(self.land0 + land + i * step, step)].astype(f32)
-
-        def to_core(self):
-            if self.index:
-                pl.semaphore_wait(credit.at[0], 1)
-            size = SUM_ROWS // 2
-            self.cast(self.other_half, size)
-            self.first = self.copy(0, self.outs(self.other_half, size), self.lands(0, size), 0, {"dp": core_mate})
-            self.first.start()
-
-        def to_x(self):
-            if self.index:
-                pl.semaphore_wait(credit.at[1], 1)
-            self.first.wait()
-            pl.semaphore_signal(ack.at[self.index, 0], inc=1, device_id={"dp": core_mate}, device_id_type=pl.DeviceIdType.MESH)
-            size = SUM_ROWS // 4
-            self.add(self.half, SUM_ROWS // 2, 0)
-            self.cast(self.other_quarter, size)
-            self.second = self.copy(
-                1, self.outs(self.other_quarter, size), self.lands(SUM_ROWS // 2, size), 1, {"dp": x_mate})
-            self.second.start()
-
-        def peers(self):
-            for q in range(8):
-                yield q, place != q, {"ty": q // 4, "tx": q % 4}
-
-        def to_group(self):
-            if self.index:
-                pl.semaphore_wait(credit.at[2], 7)
-            self.second.wait()
-            size, step = SUM_ROWS // 4, SUM_ROWS // 32
-            self.add(self.quarter, size, SUM_ROWS // 2)
-
-            @pl.loop(0, 8)
-            def _(q):
-                here = self.acc[rows16(self.quarter + step * q, step)]
-                self.land[rows16(self.land0 + step * q, step)] = here.astype(bf)
-
-            pl.semaphore_signal(ack.at[self.index, 1], inc=1, device_id={"dp": x_mate}, device_id_type=pl.DeviceIdType.MESH)
-            self.third = []
-            base = SUM_ROWS // 4 * 3
-            for q, cond, target in self.peers():
-                copy = self.copy(2 + q, self.lands(step * q, step), self.lands(base + step * place, step), 2 + place, target)
-                pl.when(cond)(copy.start)
-                self.third.append((cond, copy))
-
-        def got(self, slot, dst):
-            return self.copy(slot, dst, dst, slot, {"dp": core_mate})
-
-        def from_group(self):
-            step, base = SUM_ROWS // 32, SUM_ROWS // 4 * 3
-            for q, cond, _ in self.peers():
-                pl.when(cond)(self.got(2 + q, self.lands(base + step * q, step)).wait_recv)
-            for q, cond, _ in self.peers():
-                @pl.when(cond)
-                def _(q=q):
-                    self.acc[rows16(self.own, step)] += self.land[rows16(self.land0 + base + step * q, step)].astype(f32)
-            for cond, copy in self.third:
-                pl.when(cond)(copy.wait_send)
-            self.cast(self.own, step)
-            self.fourth = []
-            for q, cond, target in self.peers():
-                copy = self.copy(10 + q, self.outs(self.own, step), self.outs(self.own, step), 10 + place, target)
-                pl.when(cond)(copy.start)
-                self.fourth.append((cond, copy))
-
-        def back_x(self):
-            step = SUM_ROWS // 32
-            for q, cond, _ in self.peers():
-                pl.when(cond)(self.got(10 + q, self.outs(self.quarter + step * q, step)).wait_recv)
-            size = SUM_ROWS // 4
-            pl.semaphore_wait(ack.at[self.index, 1], 1)
-            self.fifth = self.copy(18, self.outs(self.quarter, size), self.outs(self.quarter, size), 18, {"dp": x_mate})
-            self.fifth.start()
-
-        def back_core(self):
-            self.got(18, self.outs(self.other_quarter, SUM_ROWS // 4)).wait_recv()
-            size = SUM_ROWS // 2
-            pl.semaphore_wait(ack.at[self.index, 0], 1)
-            self.sixth = self.copy(19, self.outs(self.half, size), self.outs(self.half, size), 19, {"dp": core_mate})
-            self.sixth.start()
-
-        def finish(self, ref, sem):
-            self.got(19, self.outs(self.other_half, SUM_ROWS // 2)).wait_recv()
-            for cond, copy in self.fourth:
-                pl.when(cond)(copy.wait_send)
-            self.fifth.wait_send()
-            self.sixth.wait_send()
-            self.store = pltpu.make_async_copy(self.outs(0, SUM_ROWS), ref, lsem.at[sem])
-            self.store.start()
+                at = start + i * self.unit
+                self.out[self.at(self.out0, at, self.unit)] = self.acc[self.at(self.acc0, at, self.unit)].astype(bf)
+
+        def step(self, k):
+            last = self.last
+            if k == 0:
+                self.send_rs(0)
+            elif k <= last:
+                self.recv_rs(k - 1)
+                self.send_rs(k)
+                self.done_rs(k - 1)
+            elif k == last + 1:
+                self.recv_rs(last)
+                n, me, target, start, chunk, land_at, sem = self.stages[last]
+                self.cast(start + me * chunk, chunk)
+                self.done_rs(last)
+                self.send_ag(last)
+            elif k <= 2 * last + 1:
+                self.recv_ag(2 * last + 2 - k)
+                self.send_ag(2 * last + 1 - k)
+            else:
+                self.recv_ag(0)
+                for s in range(last + 1):
+                    for k, cond, mine, theirs in self.near[s]:
+                        maybe(cond, lambda s=s, k=k, mine=mine, theirs=theirs: self.ag_copy(s, k, mine, theirs).wait_send())
+
+    def sums(where, at=None):
+        for (spot, spot_at), steps in SUM_PLAN.items():
+            if spot == where:
+                def go(steps=steps):
+                    for name, k in steps:
+                        totals[name].step(k)
+                        if name == "a" and k == 2 * totals[name].last + 2:
+                            pltpu.make_async_copy(outa, suma_ref, lsem.at[8]).start()
+                if at is None:
+                    go()
+                else:
+                    pl.when(at == spot_at)(go)
 
     def dot(a, b):
         return jnp.dot(a, b, preferred_element_type=f32)
@@ -742,7 +798,7 @@
         copy.start()
         return copy
 
-    eload, xload = load(ext_in, ev, 1), load(x_in, xv, 0)
+    eload, hotload, xload = load(ext_in, ev, 1), load(hot_in, slope.at[0:1152], 11), load(x_in, xv, 0)
     w1load, skipload = load(w1_in, w1, 5), load(skip_in, wskip, 6)
     cload, w2load = load(cot_in, cv, 2), load(w2_in, w2, 7)
     barrier = pltpu.get_barrier_semaphore()
@@ -768,22 +824,13 @@
         t27[f, 0] = jnp.zeros(t27.shape[2:], bf)
         t27[f, rows + 1] = jnp.zeros(t27.shape[2:], bf)
 
-    count, span = 9 * cols, cols * LANES
     eload.wait()
-    turned = cat([ev[f].astype(f32).reshape(count, rows).T for f in range(faces)], 0).astype(bf)
-
-    def packing(moves):
-        line = lax.broadcasted_iota(jnp.int32, (count, span), 0)
-        spot = lax.broadcasted_iota(jnp.int32, (count, span), 1)
-        channel, column, to_column, to_lane = line // cols, line % cols, spot // LANES, spot % LANES
-        hot = jnp.zeros((count, span), f32)
-        for start, step in moves:
-            hot = hot + jnp.where((to_lane == start + channel) & (column == to_column + step), 1.0, 0.0)
-        return hot.astype(bf)
-
-    flat = dot(turned, packing([(0, -1), (9, 0), (18, 1)]))
-    for c in range(cols):
-        pre[0, pl.ds(c * faces * rows, faces * rows)] = flat[:, c * LANES : c * LANES + LANES]
+    turned = cat([ev[f].astype(f32).reshape(9 * cols, rows).T for f in range(faces)], 0).astype(bf)
+    hotload.wait()
+    for k in range(8):
+        flat = dot(turned, slope[144 * k : 144 * k + 144])
+        for c in range(2):
+            pre[0, pl.ds((2 * k + c) * faces * rows, faces * rows)] = flat[:, c * LANES : c * LANES + LANES]
     xload.wait()
 
     @pl.loop(0, faces)
@@ -818,12 +865,18 @@
         for a in range(3):
             for b in range(3):
                 ff[h, pl.ds(128 * a + 9 * b, 9)] = w1[3 * a + b, 256:265, lanes].astype(f32)
-        ff[h, pl.ds(128 + ONE, 1)] = biases[0:1, lanes].astype(f32)
+        ff[h, pl.ds(128 + ONE, 1)] = bias_one[...].astype(f32).reshape(1, 256)[:, lanes]
         ff[h, pl.ds(384 + 9, 9)] = wskip[256:265, lanes].astype(f32)
-        ff[h, pl.ds(384 + ONE, 1)] = biases[2:3, lanes].astype(f32)
+        ff[h, pl.ds(384 + ONE, 1)] = bias_skip[...].astype(f32).reshape(1, 256)[:, lanes]
         for a in range(3):
             we[a, :, lanes] = ff[h, pl.ds(128 * a, 128)].astype(bf)
         wse[:, lanes] = ff[h, pl.ds(384, 128)].astype(bf)
+        ff[h, pl.ds(0, 256)] = jnp.zeros((256, LANES), f32)
+        for t in range(TAPS):
+            ff[h, pl.ds(9 * t, 9)] = w1[t, 256:265, lanes].astype(f32)
+        ff[h, pl.ds(128 + 36, 9)] = wskip[256:265, lanes].astype(f32)
+        for k in range(2):
+            we81[k, :, lanes] = ff[h, pl.ds(128 * k, 128)].astype(bf)
     total = 32 * faces
     spread = jnp.where(
         lax.broadcasted_iota(jnp.int32, (faces, total), 1) % faces
@@ -907,18 +960,25 @@
         rhs = cat([w_first(t) for t in range(TAPS)] + [we[a] for a in range(3)], 0)
         split(pre, (face_rows(f),), dot(lhs, rhs))
 
-    def first_part(lo, hi):
-        @pl.loop(lo, hi)
+    def first_part():
+        @pl.loop(0, faces // 2)
         def _(i):
+            pl.when(i == 3)(first.middle)
             for u in range(2):
                 fill(xc[u], xv[2 * i + u])
             for u in range(2):
                 conv_first(2 * i + u, xc[u])
 
-    first_part(0, 3)
-    first.middle()
-    first_part(3, 6)
+    first_part()
     cload.wait()
+
+    @pl.loop(0, faces // 2)
+    def _(i):
+        pair = [2 * i, 2 * i + 1]
+        field = cat([cat([xv[f].reshape(area, 256), t27[f, 1 : rows + 1].reshape(area, LANES)]) for f in pair], 0)
+        fresh = dot_tn(field, cat([cv[f] for f in pair], 0))
+        acca[2304:2560] += fresh[0:256]
+        accb[864:896] += fresh[256:288]
 
     @pl.loop(0, faces)
     def _(f):
@@ -952,9 +1012,10 @@
         rhs = cat([w2[t] for t in range(TAPS)], 0)
         split(pre, (face_rows(f),), dot(lhs, rhs))
 
-    def second_part(lo, hi):
-        @pl.loop(lo, hi)
+    def second_part():
+        @pl.loop(0, faces // 2)
         def _(i):
+            pl.when(i == 3)(second.middle)
             for u in range(2):
                 f = 2 * i + u
                 act, sl = gelu_slope(join(pre, (face_rows(f),)))
@@ -964,9 +1025,7 @@
                 conv_second(2 * i + u)
 
     w2load.wait()
-    second_part(0, 3)
-    second.middle()
-    second_part(3, 6)
+    second_part()
     second.finish()
     ring_in(second, 2)
     ring_cat(rc2v, rc2h, 2)
@@ -1036,7 +1095,7 @@
                 rhf[h, s, pl.ds(12, 384)] = v.astype(f32)
 
     def slope_two(u, h):
-        return gelu_slope(u + biases[1:2, 128 * h : 128 * h + 128].astype(f32))[1]
+        return gelu_slope(u + bias_two[...].astype(f32).reshape(1, 256)[:, 128 * h : 128 * h + 128])[1]
 
     edge_grads(
         lambda h, s: slope_two(evf[h, s], h) * cev[s, :, 128 * h : 128 * h + 128].astype(f32),
@@ -1048,61 +1107,73 @@
     def out_copy(u, f):
         return pltpu.make_async_copy(ost.at[u], out_ref.at[f], lsem.at[3 + u])
 
-    def third_part(lo, hi):
-        @pl.loop(lo, hi)
+    def third_part():
+        @pl.loop(0, faces // 2)
         def _(i):
-            grads = []
+            pl.when(i == 4)(third.middle)
+            for u in range(2):
+                out_copy(u, 0).wait()
+            grads, ready = [], []
             for u in range(2):
                 f = 2 * i + u
-                act, sl = gelu_slope(join(pre, (face_rows(f),)) + biases[1:2].astype(f32))
-                cot = cv[f]
-                grad = (cot.astype(f32) * sl).astype(bf)
-                accb[2432:2433] += jnp.sum(grad.astype(f32), axis=0, keepdims=True)
-                fill(xc[u], grad.reshape(rows, cols, 256))
+                act, sl = gelu_slope(join(pre, (face_rows(f),)) + bias_two[...].astype(f32).reshape(1, 256))
+                grad = (cv[f].astype(f32) * sl).astype(bf)
+                accb[896:897] += jnp.sum(grad.astype(f32), axis=0, keepdims=True)
                 field = cat([xv[f].reshape(area, 256), t27[f, 1 : rows + 1].reshape(area, LANES)])
                 skip = dot(field, cat([wskip[0:256], wse[...]], 0))
-                fresh = dot_tn(field, cot)
-                acca[2304:2560] += fresh[0:256]
-                accb[2400:2432] += fresh[256:288]
-
-                @pl.when(i > 0)
-                def _(u=u, f=f):
-                    out_copy(u, f).wait()
-
-                ost[u] = (act + skip).astype(bf)
-                out_copy(u, f).start()
+                ready.append((act + skip).astype(bf))
                 grads.append(grad)
+            for u in range(2):
+                cv[2 * i + u] = grads[u]
+                ost[u] = ready[u]
             pair = cat(grads, 0)
             for a in range(3):
                 field = cat([hc[2 * i + u, a : a + rows].reshape(area, 768) for u in range(2)], 0)
                 acca[768 * a : 768 * a + 768] += dot_tn(field, pair)
+            for u in range(2):
+                out_copy(u, 2 * i + u).start()
+
+    def third_back():
+        @pl.loop(0, faces // 2)
+        def _(i):
+            sums("back", i)
+            for u in range(2):
+                fill(xc[u], cv[2 * i + u].reshape(rows, cols, 256))
             rhs = cat([w2[8 - t] for t in range(TAPS)], 1)
             for u in range(2):
                 split(pre, (face_rows(2 * i + u),), dot_nt(cat(windows(xc[u])), rhs))
 
-    third_part(0, 3)
-    third.middle()
-    third_part(3, 6)
-    for u in range(2):
-        out_copy(u, 0).wait()
-
     def ring_kernel_grads(grad_ref, extra, rcv, rch):
         for s in range(2):
             fresh = dot_tn(rcv[s], gev[s])
-            grad_ref[1536 * s : 1536 * s + 768] += fresh[0:768]
+            for b in range(3):
+                at = BLOCKS[b] + 512 * s if extra else 1536 * s + 256 * b
+                grad_ref[at : at + 256] += fresh[256 * b : 256 * b + 256]
             if extra:
-                grad_ref[2304 + 64 * s : 2336 + 64 * s] += fresh[768:800]
+                grad_ref[768 + 64 * s : 800 + 64 * s] += fresh[768:800]
             fresh = dot_tn(rch[s], geh[s])
             for a in range(3):
-                t = 3 * a + 2 * s
-                grad_ref[256 * t : 256 * t + 256] += fresh[256 * a : 256 * a + 256]
+                at = BLOCKS[2 * s] + 256 * a if extra else 768 * a + 512 * s
+                grad_ref[at : at + 256] += fresh[256 * a : 256 * a + 256]
                 if extra:
-                    grad_ref[2304 + 32 * a : 2336 + 32 * a] += fresh[768 + 128 * a : 800 + 128 * a]
-
+                    grad_ref[768 + 32 * a : 800 + 32 * a] += fresh[768 + 128 * a : 800 + 128 * a]
+
+    for u in range(2):
+        ost[u] = jnp.zeros(ost.shape[1:], bf)
+        out_copy(u, u).start()
+    third_part()
     ring_kernel_grads(acca, False, rc2v, rc2h)
-    total_a = Total(0, acca, outa, 0, landa, 0)
-    total_b = Total(1, accb, slope, 3584, slope, 0)
-    total_a.to_core()
+    totals = {}
+    for index, (name, first_row, count, way) in enumerate(SUMS):
+        if name == "a":
+            totals[name] = Total(index, acca, first_row, outa, first_row, landa, first_row, count, way)
+        else:
+            totals[name] = Total(index, accb, first_row, slope, first_row, slope, 2560 + first_row, count, way)
+    sums("middle")
+    third_back()
+    for u in range(2):
+        out_copy(u, 0).wait()
+    cload = load(cot_in, cv, 2)
     third.finish()
     third.stage(2)
 
@@ -1122,104 +1193,150 @@
     edge_grads(lambda h, s: evf[h, s] * slev[h, s], lambda h, s: ehf[h, s] * sleh[h, s])
     ring_grads(fourth, w_first, 3)
     fourth.start()
-    total_a.to_x()
-
-    def fourth_part(lo, hi):
-        @pl.loop(lo, hi)
+    sums("sent")
+
+    def first_grads(f):
+        grad = (join(pre, (face_rows(f),)) * slope[face_rows(f)].astype(f32)).astype(bf)
+        fill(hc.at[f], grad.reshape(rows, cols, 256))
+
+    def shifted_grads(g, start, choose):
+        for u in range(3):
+            xc[0][1 : rows + 1, :, 256 * u : 256 * u + 256] = choose(xv[3 * g + u])
+        grads = cat([hc[3 * g + u, 1 : rows + 1, :, 256:512].reshape(area, 256) for u in range(3)], 0)
+        field = cat([
+            cat([xc[0][a : a + rows, :, 256 * u : 256 * u + 256].reshape(area, 256) for a in range(3)])
+            for u in range(3)], 0)
+        accb[pl.ds(start, 768)] += dot_tn(field, grads)
+        return grads
+
+    def fourth_start():
+        @pl.loop(0, faces // 3)
+        def _(g):
+            pl.when(g == 2)(fourth.middle)
+            for u in range(3):
+                first_grads(3 * g + u)
+            grads = shifted_grads(g, 0, lambda v: shifts(v)[0])
+            extra = cat([
+                cat([t27[3 * g + u, a : a + rows].reshape(area, LANES) for a in range(3)]) for u in range(3)], 0)
+            fresh = dot_tn(extra, grads)
+            for a in range(3):
+                accb[768 + 32 * a : 800 + 32 * a] += fresh[128 * a : 128 * a + 32]
+
+    def free_slopes():
+        for target in ({"dp": core_mate}, {"dp": x_mate}):
+            pl.semaphore_signal(credit, inc=1, device_id=target, device_id_type=pl.DeviceIdType.MESH)
+        for q in range(8):
+            @pl.when(place != q)
+            def _(q=q):
+                pl.semaphore_signal(credit, inc=1, device_id=dev(q // 4, q % 4), device_id_type=pl.DeviceIdType.MESH)
+
+    def fourth_rest():
+        @pl.loop(0, 2 * faces // 3)
         def _(i):
-            grads = []
+            b = 1 + i // 4
+            sums("more", i)
+            shifted_grads(i % 4, pl.multiple_of(256 + 768 * b, 256), lambda v: jnp.where(b == 1, v, shifts(v)[1]))
+
+    ring_kernel_grads(accb, True, rc1v, rc1h)
+    fourth_start()
+    free_slopes()
+    pl.semaphore_wait(credit, 9)
+    sums("first")
+    fourth_rest()
+    hot = landa.at[0:1152]
+    hotload = load(hot_back_in, hot, 11)
+    sums("third")
+    fourth.finish()
+    fourth.stage(3)
+
+    def part(u, j, start=0, size=area, stride=1):
+        return pl.ds((3 * u + j) * area + start, size, stride=stride)
+
+    def gx_copy(u, f):
+        return pltpu.make_async_copy(ost.at[u], gx_ref.at[f], lsem.at[3 + u])
+
+    def last_part():
+        @pl.loop(0, faces // 2)
+        def _(i):
+            sums("last", i)
+            for u in range(2):
+                gx_copy(u, 0).wait()
+            col = lax.broadcasted_iota(jnp.int32, (area, 1), 0) % cols
             for u in range(2):
                 f = 2 * i + u
-                grad = (join(pre, (face_rows(f),)) * slope[face_rows(f)].astype(f32)).astype(bf)
-                fill(hc.at[f], grad.reshape(rows, cols, 256))
-                fill(xc[u], xv[f])
-                grads.append(grad)
-            pair = cat(grads, 0)
-            for a in range(3):
-                field = cat([xc[u][a : a + rows].reshape(area, 768) for u in range(2)], 0)
-                accb[768 * a : 768 * a + 768] += dot_tn(field, pair)
-                extra = cat([t27[2 * i + u, a : a + rows].reshape(area, LANES) for u in range(2)], 0)
-                accb[2304 + 32 * a : 2336 + 32 * a] += dot_tn(extra, pair)[0:32]
-
-    fourth_part(0, 3)
-    fourth.middle()
-    total_a.to_group()
-    fourth_part(3, 6)
-    for q in range(8):
-        @pl.when(place != q)
-        def _(q=q):
-            pl.semaphore_signal(credit.at[2], inc=1, device_id=dev(q // 4, q % 4), device_id_type=pl.DeviceIdType.MESH)
-    for c, mate in ((0, core_mate), (1, x_mate)):
-        pl.semaphore_signal(credit.at[c], inc=1, device_id={"dp": mate}, device_id_type=pl.DeviceIdType.MESH)
-    ring_kernel_grads(accb, True, rc1v, rc1h)
-    total_b.to_core()
-    total_a.from_group()
-    fourth.finish()
-    fourth.stage(3)
-
-    def gx_copy(f):
-        return pltpu.make_async_copy(ost.at[f % 2], gx_ref.at[f], lsem.at[3 + f % 2])
-
-    def last_face(f):
-        cot = cv[f]
-        lhs = cat(windows(hc.at[f]) + [cot])
-        rhs = cat([w_first(8 - t) for t in range(TAPS)] + [wskip[0:256]], 1)
-        main = dot_nt(lhs, rhs)
-        for h in range(2):
-            ff[h] = main[:, 128 * h : 128 * h + 128]
-        lhs = cat([hc[f, a : a + rows, :, 256:512].reshape(area, 256) for a in range(3)] + [cot])
-        packed = dot_nt(lhs, cat([we[2], we[1], we[0], wse[...]], 1))
-        col = lax.broadcasted_iota(jnp.int32, (area, 1), 0) % cols
-        after = jnp.where(col == cols - 1, 0.0, pltpu.roll(packed, area - 1, axis=0))
-        before = jnp.where(col == 0, 0.0, pltpu.roll(packed, 1, axis=0))
-        ff[2] = after + pltpu.roll(packed, LANES - 9, axis=1) + pltpu.roll(before, LANES - 18, axis=1)
-        for j in range(3):
-            for s in range(2):
-                ff[j, pl.ds(area - cols if s else 0, cols)] += evf[j, s, ring_v(f)]
-        for j in range(3):
-            for s in range(2):
-                ff[j, pl.ds(cols - 1 if s else 0, rows, stride=cols)] += ehf[j, s, ring_h(f)]
-        for c in range(cols):
-            here = ff[2, pl.ds(c, rows, stride=cols)].astype(bf)
-            rc1h[c // 8, rows16(f * rows, rows), c % 8 * LANES : c % 8 * LANES + LANES] = here
-
-        @pl.when(f > 1)
-        def _():
-            gx_copy(f).wait()
-
-        ost[f % 2] = cat([ff[0], ff[1]]).astype(bf)
-        gx_copy(f).start()
-
-    def last_part(lo, hi):
-        @pl.loop(lo, hi)
-        def _(f):
-            last_face(f)
-
-    last_part(0, 4)
-    total_b.to_x()
-    total_a.back_x()
-    last_part(4, 8)
-    total_b.to_group()
-    total_a.back_core()
-    last_part(8, 12)
-    total_b.from_group()
-    total_a.finish(suma_ref, 8)
-    hot = packing([(0, 0)])
-    back = dot_nt(rc1h[0, :, 0 : span // 2], hot[:, 0 : span // 2]) + dot_nt(rc1h[1, :, 0 : span // 2], hot[:, span // 2 :])
+                cot = cv[f]
+                rhs = cat([w_first(8 - t) for t in range(TAPS)] + [wskip[0:256]], 1)
+                main = dot_nt(cat(windows(hc.at[f]) + [cot]), rhs)
+                for h in range(2):
+                    pre[0, part(u, h)] = main[:, 128 * h : 128 * h + 128]
+                taps = dot_nt(cat([hc[f, 1 : rows + 1, :, 256:512].reshape(area, 256), cot]), cat([we81[0], we81[1]], 1))
+                edge = jnp.zeros((cols, LANES), f32)
+                lines = (
+                    cat([taps[cols:], edge], 0)
+                    + pltpu.roll(taps, LANES - 27, axis=1)
+                    + cat([edge, pltpu.roll(taps, LANES - 54, axis=1)[: area - cols]], 0))
+                after = jnp.where(col == cols - 1, 0.0, pltpu.roll(lines, area - 1, axis=0))
+                before = jnp.where(col == 0, 0.0, pltpu.roll(lines, 1, axis=0))
+                pre[0, part(u, 2)] = after + pltpu.roll(lines, LANES - 9, axis=1) + pltpu.roll(before, LANES - 18, axis=1)
+            for u in range(2):
+                f = 2 * i + u
+                for j in range(3):
+                    for s in range(2):
+                        pre[0, part(u, j, area - cols if s else 0, cols)] += evf[j, s, ring_v(f)]
+                for j in range(3):
+                    for s in range(2):
+                        pre[0, part(u, j, cols - 1 if s else 0, rows, cols)] += ehf[j, s, ring_h(f)]
+                for c in range(cols):
+                    here = pre[0, part(u, 2, c, rows, cols)].astype(bf)
+                    rc1h[c // 8, rows16(f * rows, rows), c % 8 * LANES : c % 8 * LANES + LANES] = here
+                ost[u] = cat([pre[0, part(u, 0)], pre[0, part(u, 1)]]).astype(bf)
+            for u in range(2):
+                gx_copy(u, 2 * i + u).start()
+
+    cload.wait()
+    for u in range(2):
+        gx_copy(u, u).start()
+    last_part()
+    sums("end")
+    hotload.wait()
+    back = sum(
+        dot_nt(rc1h[k // 4, :, k % 4 * 256 : k % 4 * 256 + 256], hot[144 * k : 144 * k + 144]) for k in range(8))
     for f in range(faces):
         ev[f] = back[f * rows : f * rows + rows].T.astype(bf).reshape(9, cols, rows)
     eout = pltpu.make_async_copy(ev, gext_ref, lsem.at[1])
     eout.start()
-    total_b.back_x()
+    sums("rest")
+    stores = []
+    for a in range(3):
+        for b in range(3):
+            stores.append(pltpu.make_async_copy(
+                slope.at[pl.ds(BLOCKS[b] + 256 * a, 256)], sumb_ref.at[pl.ds(256 * (3 * a + b), 256)], lsem.at[9]))
+            stores[-1].start()
+    tail = slope[768:1024].astype(f32)
+    for t in range(TAPS):
+        tails[t] = tail[32 * (t // 3) + 9 * (t % 3) : 32 * (t // 3) + 9 * (t % 3) + 9]
+    tails[TAPS] = tail[96 + 9 : 96 + 18]
+    rests[0:1] = tail[32 + ONE : 32 + ONE + 1]
+    rests[1:2] = tail[128:129]
+    rests[2:3] = tail[96 + ONE : 96 + ONE + 1]
     for u in range(2):
-        gx_copy(u).wait()
-    total_b.back_core()
-    total_b.finish(sumb_ref, 9)
+        gx_copy(u, 0).wait()
     eout.wait()
-    total_a.store.wait()
-    total_b.store.wait()
+    pltpu.make_async_copy(outa, suma_ref, lsem.at[8]).wait()
+    pltpu.make_async_copy(slope.at[0:2304], sumb_ref, lsem.at[9]).wait()
     for ex in (first, second, third, fourth):
         ex.drain()
+
+
+def packing(extra, cols, moves):
+    hot = np.zeros((extra, cols, cols, LANES), ml_dtypes.bfloat16)
+    for start, step in moves:
+        for channel in range(extra):
+            for column in range(cols):
+                if 0 <= column - step < cols:
+                    hot[channel, column, column - step, start + channel] = 1
+    hot = hot.reshape(extra * cols, cols * LANES // 256, 256)
+    return hot.transpose(1, 0, 2).reshape(-1, 256)
 
 
 def fast_device(
@@ -1230,7 +1347,6 @@
     _, faces, rows, cols, ch = features.shape
     area = rows * cols
     extra = extra_inputs.shape[-1]
-    biases = jnp.stack([first_bias, second_bias, skip_bias])
     vm, hbm = pl.BlockSpec(memory_space=pltpu.VMEM), pl.BlockSpec(memory_space=pl.ANY)
     shape = jax.ShapeDtypeStruct
 
@@ -1246,7 +1362,8 @@
     sums = (SUM_ROWS, ch)
     scratch = [
         pltpu.VMEM((TAPS, ch + extra, ch), bf), pltpu.VMEM((TAPS, ch, ch), bf), pltpu.VMEM((ch + extra, ch), bf),
-        pltpu.VMEM((3, LANES, ch), bf), pltpu.VMEM((LANES, ch), bf), pltpu.VMEM((384, 384), bf),
+        pltpu.VMEM((3, LANES, ch), bf), pltpu.VMEM((LANES, ch), bf), pltpu.VMEM((2, LANES, ch), bf),
+        pltpu.VMEM((384, 384), bf),
         pltpu.VMEM((4, 16, LANES), f32),
         pltpu.VMEM((faces, rows, cols, ch), bf), pltpu.VMEM((faces, extra, cols, rows), bf),
         pltpu.VMEM((faces, area, ch), bf), pltpu.VMEM((faces, rows + 2, cols, LANES), bf),
@@ -1265,41 +1382,40 @@
         pltpu.VMEM(sums, f32), pltpu.VMEM(sums, f32), pltpu.VMEM(sums, bf), pltpu.VMEM(sums, bf),
         [exchange_bufs(384, 0 + 1), exchange_bufs(256, 1), exchange_bufs(256, 1), exchange_bufs(384, 1)],
         pltpu.SemaphoreType.DMA((4, 48)), pltpu.SemaphoreType.DMA((4, 33)),
-        pltpu.SemaphoreType.DMA((2, 20)), pltpu.SemaphoreType.DMA((2, 20)),
-        pltpu.SemaphoreType.REGULAR((3,)), pltpu.SemaphoreType.REGULAR((2, 2)), pltpu.SemaphoreType.DMA((10,)),
+        pltpu.SemaphoreType.DMA((len(SUMS), 20)), pltpu.SemaphoreType.DMA((len(SUMS), 20)),
+        pltpu.SemaphoreType.REGULAR, pltpu.SemaphoreType.REGULAR((len(SUMS), 4)), pltpu.SemaphoreType.DMA((12,)),
     ]
     out = pl.pallas_call(
         whole_block,
         out_shape=(
             shape((faces, area, ch), bf), shape((faces, area, ch), bf), shape((faces, extra, cols, rows), bf),
-            shape(sums, bf), shape(sums, bf),
+            shape(sums, bf), shape((TAPS * ch, ch), bf), shape((TAPS + 1, extra, ch), f32), shape((8, ch), f32),
         ),
-        in_specs=[hbm] * 5 + [vm] * 2 + [hbm],
-        out_specs=[hbm] * 5,
+        in_specs=[hbm] * 5 + [vm] * 4 + [hbm] * 3,
+        out_specs=[hbm] * 5 + [vm] * 2,
         scratch_shapes=scratch,
         compiler_params=pltpu.CompilerParams(
             collective_id=0, has_side_effects=True, vmem_limit_bytes=65400 * 1024),
     )(
         features[0], extra_inputs[0].transpose(0, 3, 2, 1), first_kernel.reshape(TAPS, ch + extra, ch),
-        second_kernel.reshape(TAPS, ch, ch), skip_kernel, biases, seam_table.transpose(1, 2, 0),
-        cotangent.reshape(faces, area, ch),
-    )
-    block_output, grad_features, grad_extra, second_sum, first_sum = out
+        second_kernel.reshape(TAPS, ch, ch), skip_kernel, first_bias, second_bias, skip_bias,
+        seam_table.transpose(1, 2, 0), cotangent.reshape(faces, area, ch),
+        packing(extra, cols, ((0, -1), (extra, 0), (2 * extra, 1))), packing(extra, cols, ((0, 0),)),
+    )
+    block_output, grad_features, grad_extra, suma, sumb, tails, rests = out
     tall = TAPS * ch
-    tail = first_sum[tall : tall + 96].reshape(3, 32, ch)
     first_grad = jnp.concatenate(
-        [first_sum[:tall].reshape(3, 3, ch, ch), tail[:, :PACK].reshape(3, 3, extra, ch)], 2)
-    skip = first_sum[tall + 96 : tall + 128]
+        [sumb.reshape(3, 3, ch, ch).astype(f32), tails[:TAPS].reshape(3, 3, extra, ch)], 2)
     return (
         block_output.reshape(features.shape),
         grad_features.reshape(features.shape),
         grad_extra.transpose(0, 3, 2, 1)[None],
-        first_grad.astype(f32),
-        tail[1, ONE].astype(f32),
-        second_sum[:tall].reshape(3, 3, ch, ch).astype(f32),
-        first_sum[tall + 128].astype(f32),
-        jnp.concatenate([second_sum[tall:], skip[extra : 2 * extra]], 0).astype(f32),
-        skip[ONE].astype(f32),
+        first_grad,
+        rests[0],
+        suma[:tall].astype(f32).reshape(second_kernel.shape),
+        rests[1],
+        jnp.concatenate([suma[tall:].astype(f32), tails[TAPS]], 0),
+        rests[2],
     )
 
 

time: 174 us -> 162 us (0.931)
  Pallas kernels: 155 us -> 146 us
  local copies, waits for them, and re-layouts: 11.5 us -> 8.72 us
    pallas_call x1, Pallas kernels: 155 us -> 146 us  [fast_device(): pl.pallas_call(whole_block, out_shape=(shape((faces, area, ch), bf), shap...]
    convert_element_type x5 -> x2, other arithmetic: 5.96 us -> 1.5 us  [the longest x1 1.48 us: fast_device(): sumb.reshape(3, 3, ch, ch).astype(f32)]
    concatenate x0 -> x2, other arithmetic: none -> 2.37 us  [the longest x1 1.64 us: fast_device(): jnp.concatenate([sumb.reshape(3, 3, ch, ch).astype(f32), tails[:TAPS].res...]
    another operation x3 -> x0, local copies, waits for them, and re-layouts: 1.98 us -> none  [fast_device(): biases = jnp.stack([first_bias, second_bias, skip_bias])]
where the time goes in v2:
time: 162 us; the launch traced here: 161 us
  Pallas kernels  146 us (90%)
  local copies, waits for them, and re-layouts  8.72 us (5%)
  other arithmetic  5.5 us (3%)
    pallas_call x1, Pallas kernels, fast_device(): pl.pallas_call(whole_block, out_shape=(shape((faces, area, ch), bf), shap...  146 us
    unnamed x11, local copies, waits for them, and re-layouts  5.46 us

profile of v2, /device:TPU:0, one launch (start us, length us, event | category | flops | bytes accessed | tf_op | source)
XLA Modules:
  0.0 161.1 jit_solution(869217896764669811)
XLA Ops:
  0.6 146.2 %shard_map.187 = (bf16[12,512,256]{2,1,0:T(8,128)(2,1)}, bf16[12,512,256]{2,1,0:T(8,128)(2,1)}, bf16[12,9,16,32]{3,2,1,0:T(8,128)(2,1)}, bf16[2560,256]{1,0:T(8,...) custom-call(bf16[12,32,16,256]{3,2,1,0:T(8,128)(2,1)} %bitcast.26, ...), custom_call_target="tpu_custom_call" | custom-call | tf_op jit(solution)/shard_map/pallas_call | solution.py:1388
  146.9 0.9 slice.21
  147.8 1.5 convert.2
  149.3 0.0 copy-start.2
  149.3 1.6 %pad_maximum_fusion = f32[3,3,265,256]{3,2,1,0:T(8,128)} fusion(f32[3,3,9,256]{3,2,1,0:T(8,128)S(1)} %bitcast.31, f32[3,3,256,256]{3,2,1,0:T(8,128)S(1)} %convert.2), kind=kLoop, calls=%fused_computation | loop fusion | flops 610560 | bytes 4884480 | tf_op jit(solution)/shard_map/concatenate | solution.py:1407
  150.9 1.4 fusion
  152.3 0.0 copy-done.2
  152.3 0.1 slice.23
  152.4 0.0 copy-start.1
  152.4 1.6 %convert.3 = f32[3,3,256,256]{3,2,1,0:T(8,128)} convert(bf16[3,3,256,256]{3,2,1,0:T(8,128)(2,1)S(1)} %bitcast.23) | non-fusion elementwise | flops 589824 | bytes 3538944 | tf_op jit(solution)/shard_map/reshape | solution.py:1415
  154.0 0.9 slice_bitcast_fusion
  154.9 0.7 pad_maximum_fusion.1
  155.7 0.0 copy-done.1
  155.7 0.0 copy-start
  155.7 1.7 %copy.24 = bf16[1,12,32,16,256]{4,3,2,1,0:T(8,128)(2,1)} copy(bf16[1,12,32,16,256]{4,3,2,1,0:T(8,128)(2,1)S(1)} %bitcast.25) | data formatting | bytes 6291456
  157.3 1.4 copy-done
  158.7 0.0 copy-start.3
  158.7 1.7 %copy.25 = bf16[1,12,32,16,256]{4,3,2,1,0:T(8,128)(2,1)} copy(bf16[1,12,32,16,256]{4,3,2,1,0:T(8,128)(2,1)S(1)} %bitcast.24) | data formatting | bytes 6291456
  160.4 0.0 copy-done.3
  160.4 0.8 copy.26
  (1 shorter events, 0.0 us)
Async XLA Ops:
  149.3 3.0 %copy-start.2 = (bf16[2560,256]{1,0:T(8,128)(2,1)S(1)}, bf16[2560,256]{1,0:T(8,128)(2,1)}, u32[]{:S(2)}) copy-start(bf16[2560,256]{1,0:T(8,128)(2,1)} %get-tuple-element.22) | copy-start | bytes 3932164
  152.4 3.3 %copy-start.1 = (bf16[12,512,256]{2,1,0:T(8,128)(2,1)S(1)}, bf16[12,512,256]{2,1,0:T(8,128)(2,1)}, u32[]{:S(2)}) copy-start(bf16[12,512,256]{2,1,0:T(8,128)(2,1)} %get-tuple-element.16) | copy-start | bytes 9437188
  155.7 3.0 %copy-start = (bf16[12,512,256]{2,1,0:T(8,128)(2,1)S(1)}, bf16[12,512,256]{2,1,0:T(8,128)(2,1)}, u32[]{:S(2)}) copy-start(bf16[12,512,256]{2,1,0:T(8,128)(2,1)} %get-tuple-element.17) | copy-start | bytes 9437188
  158.7 1.7 %copy-start.3 = (bf16[12,9,16,32]{3,2,1,0:T(8,128)(2,1)S(1)}, bf16[12,9,16,32]{3,2,1,0:T(8,128)(2,1)}, u32[]{:S(2)}) copy-start(bf16[12,9,16,32]{3,2,1,0:T(8,128)(2,1)} %get-tuple-element.18) | copy-start | bytes 331780

commit v3 on v2

--- a/solution.py
+++ b/solution.py
@@ -292,33 +292,36 @@
 PACK = 27
 ONE = 27
 FOUR = ("core", "x", "y", "z")
-THREE = ("core", "x", "yz")
-SUMS = (("a", 0, 2560, FOUR), ("b", 0, 1024, THREE), ("c", 1024, 512, THREE), ("d", 1536, 512, THREE), ("e", 2048, 512, THREE))
+FOURY = ("core", "y", "x", "z")
+SUMS = (("a", 0, 2560, FOUR), ("b", 0, 1024, FOUR), ("c", 1024, 512, FOURY), ("d", 1536, 1024, FOURY))
 BLOCKS = (0, 1024, 1792)
 SUM_PLAN = {
-    ("middle", 0): (("a", 0),),
-    ("back", 2): (("a", 1),),
-    ("sent", 0): (("a", 2),),
-    ("first", 0): (("b", 0), ("a", 3)),
-    ("more", 4): (("c", 0), ("b", 1)),
-    ("more", 6): (("a", 4),),
-    ("third", 0): (("d", 0), ("e", 0), ("c", 1)),
-    ("last", 1): (("d", 1), ("e", 1), ("b", 2), ("a", 5)),
-    ("last", 2): (("c", 2),),
-    ("last", 3): (("d", 2), ("e", 2), ("b", 3), ("a", 6)),
-    ("last", 4): (("c", 3),),
-    ("last", 5): (("d", 3), ("e", 3), ("b", 4)),
-    ("end", 0): (("c", 4), ("a", 7), ("d", 4), ("e", 4), ("b", 5)),
-    ("rest", 0): (("c", 5), ("d", 5), ("e", 5), ("a", 8), ("b", 6), ("c", 6), ("d", 6), ("e", 6)),
+    ('middle', 0): (('a', 0),),
+    ('back', 4): (('a', 1),),
+    ('sent', 0): (('a', 2),),
+    ('first', 0): (('b', 0),),
+    ('more', 4): (('b', 1), ('c', 0)),
+    ('third', 0): (('a', 3), ('c', 1), ('d', 0)),
+    ('out', 2): (('b', 2),),
+    ('out', 3): (('d', 1),),
+    ('out', 5): (('c', 2),),
+    ('last', 0): (('a', 4), ('b', 3), ('d', 2)),
+    ('last', 1): (('c', 3), ('d', 3)),
+    ('last', 2): (('a', 5), ('b', 4), ('c', 4), ('d', 4)),
+    ('last', 3): (('b', 5), ('c', 5), ('d', 5)),
+    ('last', 4): (('a', 6), ('b', 6), ('c', 6)),
+    ('last', 5): (('c', 7), ('d', 6)),
+    ('end', 0): (('a', 7), ('b', 7), ('c', 8), ('d', 7)),
+    ('rest', 0): (('a', 8), ('b', 8), ('d', 8)),
 }
 
 
 def whole_block(
     x_in, ext_in, w1_in, w2_in, skip_in, bias_one, bias_two, bias_skip, table, cot_in, hot_in, hot_back_in,
-    out_ref, gx_ref, gext_ref, suma_ref, sumb_ref, tails, rests,
-    w1, w2, wskip, we, wse, we81, sel_t, rule,
+    out_ref, gx_ref, gext_ref, second_ref, first_ref, kept, skip_ref, one_ref, two_ref, three_ref,
+    w1, w2, wskip, we, wse, we81, sel_t, rule, tails,
     xv, ev, cv, t27, xc, hc, pre, slope, slev, sleh, cev, ceh,
-    ost, ff, evf, ehf, rvf, rhf, cvf, chf, rc1v, rc1h, rc2v, rc2h, gev, geh,
+    ff, evf, ehf, rvf, rhf, cvf, chf, rc1v, rc1h, rc2v, rc2h, gev, geh,
     acca, accb, outa, landa, bufs, ssem, rsem, sum_ssem, sum_rsem, credit, ack, lsem,
 ):
     f32, bf = jnp.float32, jnp.bfloat16
@@ -730,8 +733,6 @@
                 def go(steps=steps):
                     for name, k in steps:
                         totals[name].step(k)
-                        if name == "a" and k == 2 * totals[name].last + 2:
-                            pltpu.make_async_copy(outa, suma_ref, lsem.at[8]).start()
                 if at is None:
                     go()
                 else:
@@ -963,13 +964,12 @@
     def first_part():
         @pl.loop(0, faces // 2)
         def _(i):
-            pl.when(i == 3)(first.middle)
+            pl.when(i == 2)(first.middle)
             for u in range(2):
                 fill(xc[u], xv[2 * i + u])
             for u in range(2):
                 conv_first(2 * i + u, xc[u])
 
-    first_part()
     cload.wait()
 
     @pl.loop(0, faces // 2)
@@ -991,6 +991,7 @@
     for s in range(2):
         cev[s] = join(cvf, (s,)).astype(bf)
         ceh[s] = join(chf, (s,)).astype(bf)
+    first_part()
     first.finish()
     ring_in(first, 3)
     ring_cat(rc1v, rc1h, 3)
@@ -1104,34 +1105,45 @@
     ring_grads(third, lambda t: w2[t], 2)
     third.start()
 
-    def out_copy(u, f):
-        return pltpu.make_async_copy(ost.at[u], out_ref.at[f], lsem.at[3 + u])
+    def out_copy(f):
+        return pltpu.make_async_copy(hc.at[f, pl.ds(1, rows), :, pl.ds(0, 256)], out_ref.at[f], lsem.at[3])
+
+    def gx_copy(f):
+        return pltpu.make_async_copy(hc.at[f, pl.ds(1, rows), :, pl.ds(512, 256)], gx_ref.at[f], lsem.at[4])
+
+    def second_bias():
+        return bias_two[...].astype(f32).reshape(1, 256)
 
     def third_part():
         @pl.loop(0, faces // 2)
         def _(i):
             pl.when(i == 4)(third.middle)
-            for u in range(2):
-                out_copy(u, 0).wait()
-            grads, ready = [], []
+            grads = []
             for u in range(2):
                 f = 2 * i + u
-                act, sl = gelu_slope(join(pre, (face_rows(f),)) + bias_two[...].astype(f32).reshape(1, 256))
+                sl = gelu_slope(join(pre, (face_rows(f),)) + second_bias())[1]
                 grad = (cv[f].astype(f32) * sl).astype(bf)
                 accb[896:897] += jnp.sum(grad.astype(f32), axis=0, keepdims=True)
-                field = cat([xv[f].reshape(area, 256), t27[f, 1 : rows + 1].reshape(area, LANES)])
-                skip = dot(field, cat([wskip[0:256], wse[...]], 0))
-                ready.append((act + skip).astype(bf))
                 grads.append(grad)
             for u in range(2):
                 cv[2 * i + u] = grads[u]
-                ost[u] = ready[u]
             pair = cat(grads, 0)
             for a in range(3):
                 field = cat([hc[2 * i + u, a : a + rows].reshape(area, 768) for u in range(2)], 0)
                 acca[768 * a : 768 * a + 768] += dot_tn(field, pair)
+
+    def output_part():
+        @pl.loop(0, faces // 2)
+        def _(i):
+            sums("out", i)
             for u in range(2):
-                out_copy(u, 2 * i + u).start()
+                f = 2 * i + u
+                act = gelu_slope(join(pre, (face_rows(f),)) + second_bias())[0]
+                field = cat([xv[f].reshape(area, 256), t27[f, 1 : rows + 1].reshape(area, LANES)])
+                whole = (act + dot(field, cat([wskip[0:256], wse[...]], 0))).astype(bf)
+                hc[f, 1 : rows + 1, :, 0:256] = whole.reshape(rows, cols, 256)
+            for u in range(2):
+                out_copy(2 * i + u).start()
 
     def third_back():
         @pl.loop(0, faces // 2)
@@ -1158,21 +1170,18 @@
                 if extra:
                     grad_ref[768 + 32 * a : 800 + 32 * a] += fresh[768 + 128 * a : 800 + 128 * a]
 
-    for u in range(2):
-        ost[u] = jnp.zeros(ost.shape[1:], bf)
-        out_copy(u, u).start()
+    keep = load(pre, kept, 12)
     third_part()
+    keep.wait()
     ring_kernel_grads(acca, False, rc2v, rc2h)
     totals = {}
     for index, (name, first_row, count, way) in enumerate(SUMS):
-        if name == "a":
+        if name[0] == "a":
             totals[name] = Total(index, acca, first_row, outa, first_row, landa, first_row, count, way)
         else:
             totals[name] = Total(index, accb, first_row, slope, first_row, slope, 2560 + first_row, count, way)
     sums("middle")
     third_back()
-    for u in range(2):
-        out_copy(u, 0).wait()
     cload = load(cot_in, cv, 2)
     third.finish()
     third.stage(2)
@@ -1197,7 +1206,7 @@
 
     def first_grads(f):
         grad = (join(pre, (face_rows(f),)) * slope[face_rows(f)].astype(f32)).astype(bf)
-        fill(hc.at[f], grad.reshape(rows, cols, 256))
+        hc[f, 1 : rows + 1, :, 256:512] = grad.reshape(rows, cols, 256)
 
     def shifted_grads(g, start, choose):
         for u in range(3):
@@ -1212,7 +1221,6 @@
     def fourth_start():
         @pl.loop(0, faces // 3)
         def _(g):
-            pl.when(g == 2)(fourth.middle)
             for u in range(3):
                 first_grads(3 * g + u)
             grads = shifted_grads(g, 0, lambda v: shifts(v)[0])
@@ -1234,6 +1242,7 @@
         @pl.loop(0, 2 * faces // 3)
         def _(i):
             b = 1 + i // 4
+            pl.when(i == 2)(fourth.middle)
             sums("more", i)
             shifted_grads(i % 4, pl.multiple_of(256 + 768 * b, 256), lambda v: jnp.where(b == 1, v, shifts(v)[1]))
 
@@ -1242,31 +1251,30 @@
     free_slopes()
     pl.semaphore_wait(credit, 9)
     sums("first")
+    keep = load(kept, pre, 12)
     fourth_rest()
     hot = landa.at[0:1152]
     hotload = load(hot_back_in, hot, 11)
     sums("third")
+    keep.wait()
+    output_part()
     fourth.finish()
     fourth.stage(3)
 
     def part(u, j, start=0, size=area, stride=1):
         return pl.ds((3 * u + j) * area + start, size, stride=stride)
-
-    def gx_copy(u, f):
-        return pltpu.make_async_copy(ost.at[u], gx_ref.at[f], lsem.at[3 + u])
 
     def last_part():
         @pl.loop(0, faces // 2)
         def _(i):
             sums("last", i)
-            for u in range(2):
-                gx_copy(u, 0).wait()
             col = lax.broadcasted_iota(jnp.int32, (area, 1), 0) % cols
             for u in range(2):
                 f = 2 * i + u
                 cot = cv[f]
                 rhs = cat([w_first(8 - t) for t in range(TAPS)] + [wskip[0:256]], 1)
-                main = dot_nt(cat(windows(hc.at[f]) + [cot]), rhs)
+                fill(xc[u], hc[f, 1 : rows + 1, :, 256:512])
+                main = dot_nt(cat(windows(xc[u]) + [cot]), rhs)
                 for h in range(2):
                     pre[0, part(u, h)] = main[:, 128 * h : 128 * h + 128]
                 taps = dot_nt(cat([hc[f, 1 : rows + 1, :, 256:512].reshape(area, 256), cot]), cat([we81[0], we81[1]], 1))
@@ -1289,13 +1297,12 @@
                 for c in range(cols):
                     here = pre[0, part(u, 2, c, rows, cols)].astype(bf)
                     rc1h[c // 8, rows16(f * rows, rows), c % 8 * LANES : c % 8 * LANES + LANES] = here
-                ost[u] = cat([pre[0, part(u, 0)], pre[0, part(u, 1)]]).astype(bf)
+                whole = cat([pre[0, part(u, 0)], pre[0, part(u, 1)]]).astype(bf)
+                hc[f, 1 : rows + 1, :, 512:768] = whole.reshape(rows, cols, 256)
             for u in range(2):
-                gx_copy(u, 2 * i + u).start()
+                gx_copy(2 * i + u).start()
 
     cload.wait()
-    for u in range(2):
-        gx_copy(u, u).start()
     last_part()
     sums("end")
     hotload.wait()
@@ -1306,24 +1313,38 @@
     eout = pltpu.make_async_copy(ev, gext_ref, lsem.at[1])
     eout.start()
     sums("rest")
-    stores = []
-    for a in range(3):
-        for b in range(3):
-            stores.append(pltpu.make_async_copy(
-                slope.at[pl.ds(BLOCKS[b] + 256 * a, 256)], sumb_ref.at[pl.ds(256 * (3 * a + b), 256)], lsem.at[9]))
-            stores[-1].start()
     tail = slope[768:1024].astype(f32)
+    for h in range(2):
+        for t in range(TAPS):
+            at = 32 * (t // 3) + 9 * (t % 3)
+            tails[t, :, 128 * h : 128 * h + 128] = tail[at : at + 9, 128 * h : 128 * h + 128]
     for t in range(TAPS):
-        tails[t] = tail[32 * (t // 3) + 9 * (t % 3) : 32 * (t // 3) + 9 * (t % 3) + 9]
-    tails[TAPS] = tail[96 + 9 : 96 + 18]
-    rests[0:1] = tail[32 + ONE : 32 + ONE + 1]
-    rests[1:2] = tail[128:129]
-    rests[2:3] = tail[96 + ONE : 96 + ONE + 1]
-    for u in range(2):
-        gx_copy(u, 0).wait()
+        pltpu.make_async_copy(tails.at[t], first_ref.at[t, pl.ds(256, 9)], lsem.at[10]).start()
+    for b in range(3):
+        @pl.loop(0, 3)
+        def _(a):
+            accb[pl.ds(pl.multiple_of(BLOCKS[b] + 256 * a, 256), 256)] = slope[
+                pl.ds(pl.multiple_of(BLOCKS[b] + 256 * a, 256), 256)].astype(f32)
+            pltpu.make_async_copy(
+                accb.at[pl.ds(pl.multiple_of(BLOCKS[b] + 256 * a, 256), 256)], first_ref.at[3 * a + b, pl.ds(0, 256)],
+                lsem.at[9]).start()
+    @pl.loop(0, TAPS)
+    def _(t):
+        here = pl.ds(pl.multiple_of(256 * t, 256), 256)
+        acca[here] = outa[here].astype(f32)
+        pltpu.make_async_copy(acca.at[here], second_ref.at[here], lsem.at[8]).start()
+
+    skip_ref[0:256] = outa[2304:2560].astype(f32)
+    skip_ref[256:265] = tail[96 + 9 : 96 + 18]
+    one_ref[...] = tail[32 + ONE : 32 + ONE + 1]
+    two_ref[...] = tail[128:129]
+    three_ref[...] = tail[96 + ONE : 96 + ONE + 1]
+    pltpu.make_async_copy(out_ref, out_ref, lsem.at[3]).wait()
+    pltpu.make_async_copy(gx_ref, gx_ref, lsem.at[4]).wait()
     eout.wait()
-    pltpu.make_async_copy(outa, suma_ref, lsem.at[8]).wait()
-    pltpu.make_async_copy(slope.at[0:2304], sumb_ref, lsem.at[9]).wait()
+    pltpu.make_async_copy(acca.at[0:2304], second_ref, lsem.at[8]).wait()
+    pltpu.make_async_copy(accb.at[0:2304], accb.at[0:2304], lsem.at[9]).wait()
+    pltpu.make_async_copy(tails, tails, lsem.at[10]).wait()
     for ex in (first, second, third, fourth):
         ex.drain()
 
@@ -1364,14 +1385,13 @@
         pltpu.VMEM((TAPS, ch + extra, ch), bf), pltpu.VMEM((TAPS, ch, ch), bf), pltpu.VMEM((ch + extra, ch), bf),
         pltpu.VMEM((3, LANES, ch), bf), pltpu.VMEM((LANES, ch), bf), pltpu.VMEM((2, LANES, ch), bf),
         pltpu.VMEM((384, 384), bf),
-        pltpu.VMEM((4, 16, LANES), f32),
+        pltpu.VMEM((4, 16, LANES), f32), pltpu.VMEM((TAPS, extra, ch), f32),
         pltpu.VMEM((faces, rows, cols, ch), bf), pltpu.VMEM((faces, extra, cols, rows), bf),
         pltpu.VMEM((faces, area, ch), bf), pltpu.VMEM((faces, rows + 2, cols, LANES), bf),
         [pltpu.VMEM(cat_shape, bf)] * 2, pltpu.VMEM((faces,) + cat_shape, bf),
         pltpu.VMEM((2, faces * area, LANES), f32), pltpu.VMEM((faces * area, ch), bf),
         pltpu.VMEM((2, 2, 192, LANES), f32), pltpu.VMEM((2, 2, 384, LANES), f32),
         pltpu.VMEM((2, 192, ch), bf), pltpu.VMEM((2, 384, ch), bf),
-        pltpu.VMEM((2, area, ch), bf),
         pltpu.VMEM((3, area, LANES), f32),
         pltpu.VMEM((3, 2, 192, LANES), f32), pltpu.VMEM((3, 2, 384, LANES), f32),
         pltpu.VMEM((3, 2, 240, LANES), f32), pltpu.VMEM((3, 2, 408, LANES), f32),
@@ -1383,16 +1403,18 @@
         [exchange_bufs(384, 0 + 1), exchange_bufs(256, 1), exchange_bufs(256, 1), exchange_bufs(384, 1)],
         pltpu.SemaphoreType.DMA((4, 48)), pltpu.SemaphoreType.DMA((4, 33)),
         pltpu.SemaphoreType.DMA((len(SUMS), 20)), pltpu.SemaphoreType.DMA((len(SUMS), 20)),
-        pltpu.SemaphoreType.REGULAR, pltpu.SemaphoreType.REGULAR((len(SUMS), 4)), pltpu.SemaphoreType.DMA((12,)),
+        pltpu.SemaphoreType.REGULAR, pltpu.SemaphoreType.REGULAR((len(SUMS), 4)), pltpu.SemaphoreType.DMA((13,)),
     ]
     out = pl.pallas_call(
         whole_block,
         out_shape=(
-            shape((faces, area, ch), bf), shape((faces, area, ch), bf), shape((faces, extra, cols, rows), bf),
-            shape(sums, bf), shape((TAPS * ch, ch), bf), shape((TAPS + 1, extra, ch), f32), shape((8, ch), f32),
+            shape((faces, rows, cols, ch), bf), shape((faces, rows, cols, ch), bf), shape((faces, extra, cols, rows), bf),
+            shape((TAPS * ch, ch), f32), shape((TAPS, ch + extra, ch), f32),
+            shape((2, faces * area, LANES), f32), shape((ch + extra, ch), f32),
+            shape((1, ch), f32), shape((1, ch), f32), shape((1, ch), f32),
         ),
         in_specs=[hbm] * 5 + [vm] * 4 + [hbm] * 3,
-        out_specs=[hbm] * 5 + [vm] * 2,
+        out_specs=[hbm] * 6 + [vm] * 4,
         scratch_shapes=scratch,
         compiler_params=pltpu.CompilerParams(
             collective_id=0, has_side_effects=True, vmem_limit_bytes=65400 * 1024),
@@ -1402,20 +1424,17 @@
         seam_table.transpose(1, 2, 0), cotangent.reshape(faces, area, ch),
         packing(extra, cols, ((0, -1), (extra, 0), (2 * extra, 1))), packing(extra, cols, ((0, 0),)),
     )
-    block_output, grad_features, grad_extra, suma, sumb, tails, rests = out
-    tall = TAPS * ch
-    first_grad = jnp.concatenate(
-        [sumb.reshape(3, 3, ch, ch).astype(f32), tails[:TAPS].reshape(3, 3, extra, ch)], 2)
+    block_output, grad_features, grad_extra, second_grad, first_grad, _, skip_grad, one, two, three = out
     return (
         block_output.reshape(features.shape),
         grad_features.reshape(features.shape),
         grad_extra.transpose(0, 3, 2, 1)[None],
-        first_grad,
-        rests[0],
-        suma[:tall].astype(f32).reshape(second_kernel.shape),
-        rests[1],
-        jnp.concatenate([suma[tall:].astype(f32), tails[TAPS]], 0),
-        rests[2],
+        first_grad.reshape(first_kernel.shape),
+        one[0],
+        second_grad.reshape(second_kernel.shape),
+        two[0],
+        skip_grad,
+        three[0],
     )
 
 

time: 162 us -> 150 us (0.926)
  Pallas kernels: 146 us -> 137 us
  other arithmetic: 5.5 us -> 0 us
  local copies, waits for them, and re-layouts: 8.72 us -> 12.3 us
    pallas_call x1, Pallas kernels: 146 us -> 137 us  [fast_device(): pl.pallas_call(whole_block, out_shape=(shape((faces, rows, cols, ch), bf)...]
    unnamed x11 -> x25, local copies, waits for them, and re-layouts: 5.46 us -> 12.3 us
    slice x3 -> x0, local copies, waits for them, and re-layouts: 2.38 us -> none  [the longest x1 1.38 us: fast_device(): rests[2]]
    concatenate x2 -> x0, other arithmetic: 2.37 us -> none  [the longest x1 1.64 us: fast_device(): jnp.concatenate([sumb.reshape(3, 3, ch, ch).astype(f32), tails[:TAPS].res...]
    reshape x1 -> x0, other arithmetic: 1.63 us -> none  [fast_device(): suma[:tall].astype(f32).reshape(second_kernel.shape)]
where the time goes in v3:
time: 150 us
  Pallas kernels  137 us (91%)
  local copies, waits for them, and re-layouts  12.3 us (8%)
    pallas_call x1, Pallas kernels, fast_device(): pl.pallas_call(whole_block, out_shape=(shape((faces, rows, cols, ch), bf)...  137 us
    unnamed x25, local copies, waits for them, and re-layouts  12.3 us

profile of v3, /device:TPU:0, one launch (start us, length us, event | category | flops | bytes accessed | tf_op | source)
XLA Modules:
  0.0 150.0 jit_solution(6208024317790792631)
XLA Ops:
  0.6 137.0 %shard_map.187 = (bf16[12,32,16,256]{3,2,1,0:T(8,128)(2,1)}, bf16[12,32,16,256]{3,2,1,0:T(8,128)(2,1)}, bf16[12,9,16,32]{3,2,1,0:T(8,128)(2,1)}, f32[2304,256]{1...) custom-call(bf16[12,32,16,256]{3,2,1,0:T(8,128)(2,1)} %bitcast.20, ...), custom_call_target="tpu_custom_call" | custom-call | tf_op jit(solution)/shard_map/pallas_call | solution.py:1408
  137.7 0.0 copy-start
  137.7 3.9 %copy.30 = bf16[1,12,32,16,256]{4,3,2,1,0:T(8,128)(2,1)} copy(bf16[1,12,32,16,256]{4,3,2,1,0:T(8,128)(2,1)} %bitcast.19) | data formatting | bytes 6291456
  141.6 0.0 copy-done
  141.6 0.0 copy-start.3
  141.6 0.0 copy-start.1
  141.6 1.7 %copy.31 = bf16[1,12,32,16,256]{4,3,2,1,0:T(8,128)(2,1)} copy(bf16[1,12,32,16,256]{4,3,2,1,0:T(8,128)(2,1)S(1)} %bitcast.18) | data formatting | bytes 6291456
  143.3 0.0 copy-done.3
  143.3 0.0 copy-start.7
  143.3 0.0 copy-start.2
  143.3 0.8 copy.32
  144.0 0.7 copy-done.1
  144.8 1.5 copy.33
  146.2 0.0 copy-done.7
  146.2 0.0 copy-start.6
  146.2 0.6 copy.34
  146.8 0.0 copy-done.2
  146.8 1.4 copy.35
  148.2 0.0 copy-done.6
  148.2 0.6 copy.36
  148.8 0.0 copy-done.4
  148.8 0.7 copy.37
  149.5 0.0 copy-done.5
  149.5 0.6 copy.38
  (2 shorter events, 0.0 us)
Async XLA Ops:
  137.7 3.9 %copy-start = (bf16[12,32,16,256]{3,2,1,0:T(8,128)(2,1)S(1)}, bf16[12,32,16,256]{3,2,1,0:T(8,128)(2,1)}, u32[]{:S(2)}) copy-start(bf16[12,32,16,256]{3,2,1,0:T(8,128)(2,1)} %get-tuple-element.19) | copy-start | bytes 9437188
  141.6 1.7 %copy-start.3 = (bf16[12,9,16,32]{3,2,1,0:T(8,128)(2,1)S(1)}, bf16[12,9,16,32]{3,2,1,0:T(8,128)(2,1)}, u32[]{:S(2)}) copy-start(bf16[12,9,16,32]{3,2,1,0:T(8,128)(2,1)} %get-tuple-element.20) | copy-start | bytes 331780
  141.6 3.2 %copy-start.1 = (f32[9,265,256]{2,1,0:T(8,128)S(1)}, f32[9,265,256]{2,1,0:T(8,128)}, u32[]{:S(2)}) copy-start(f32[9,265,256]{2,1,0:T(8,128)} %get-tuple-element.21) | copy-start | bytes 7326724
  143.3 2.9 %copy-start.7 = (f32[1,256]{1,0:T(1,128)S(1)}, f32[1,256]{1,0:T(1,128)}, u32[]{:S(2)}) copy-start(f32[1,256]{1,0:T(1,128)} %get-tuple-element.22) | copy-start | bytes 3076
  143.3 3.5 %copy-start.2 = (f32[2304,256]{1,0:T(8,128)S(1)}, f32[2304,256]{1,0:T(8,128)}, u32[]{:S(2)}) copy-start(f32[2304,256]{1,0:T(8,128)} %get-tuple-element.23) | copy-start | bytes 7077892
  146.2 2.0 %copy-start.6 = (f32[1,256]{1,0:T(1,128)S(1)}, f32[1,256]{1,0:T(1,128)}, u32[]{:S(2)}) copy-start(f32[1,256]{1,0:T(1,128)} %get-tuple-element.24) | copy-start | bytes 3076
  146.2 2.5 %copy-start.4 = (f32[265,256]{1,0:T(8,128)S(1)}, f32[265,256]{1,0:T(8,128)}, u32[]{:S(2)}) copy-start(f32[265,256]{1,0:T(8,128)} %get-tuple-element.43) | copy-start | bytes 814084
  146.2 3.3 %copy-start.5 = (f32[1,256]{1,0:T(1,128)S(1)}, f32[1,256]{1,0:T(1,128)}, u32[]{:S(2)}) copy-start(f32[1,256]{1,0:T(1,128)} %get-tuple-element.26) | copy-start | bytes 3076

commit v4 on v3

--- a/solution.py
+++ b/solution.py
@@ -300,19 +300,19 @@
     ('back', 4): (('a', 1),),
     ('sent', 0): (('a', 2),),
     ('first', 0): (('b', 0),),
-    ('more', 4): (('b', 1), ('c', 0)),
-    ('third', 0): (('a', 3), ('c', 1), ('d', 0)),
+    ('more', 4): (('c', 0), ('b', 1)),
+    ('third', 0): (('d', 0), ('c', 1), ('a', 3)),
     ('out', 2): (('b', 2),),
     ('out', 3): (('d', 1),),
     ('out', 5): (('c', 2),),
-    ('last', 0): (('a', 4), ('b', 3), ('d', 2)),
-    ('last', 1): (('c', 3), ('d', 3)),
-    ('last', 2): (('a', 5), ('b', 4), ('c', 4), ('d', 4)),
-    ('last', 3): (('b', 5), ('c', 5), ('d', 5)),
-    ('last', 4): (('a', 6), ('b', 6), ('c', 6)),
-    ('last', 5): (('c', 7), ('d', 6)),
-    ('end', 0): (('a', 7), ('b', 7), ('c', 8), ('d', 7)),
-    ('rest', 0): (('a', 8), ('b', 8), ('d', 8)),
+    ('last', 0): (('d', 2), ('b', 3), ('a', 4)),
+    ('last', 1): (('d', 3), ('c', 3)),
+    ('last', 2): (('d', 4), ('c', 4), ('b', 4), ('a', 5)),
+    ('last', 3): (('d', 5), ('c', 5), ('b', 5)),
+    ('last', 4): (('c', 6), ('b', 6), ('a', 6)),
+    ('last', 5): (('d', 6), ('c', 7)),
+    ('end', 0): (('d', 7), ('c', 8), ('b', 7), ('a', 7)),
+    ('rest', 0): (('d', 8), ('b', 8), ('a', 8)),
 }
 
 
@@ -964,7 +964,7 @@
     def first_part():
         @pl.loop(0, faces // 2)
         def _(i):
-            pl.when(i == 2)(first.middle)
+            pl.when(i == 3)(first.middle)
             for u in range(2):
                 fill(xc[u], xv[2 * i + u])
             for u in range(2):

time: 150 us -> 153 us (1.020)
  Pallas kernels: 137 us -> 140 us
    pallas_call x1, Pallas kernels: 137 us -> 140 us  [fast_device(): pl.pallas_call(whole_block, out_shape=(shape((faces, rows, cols, ch), bf)...]
where the time goes in v4:
time: 153 us
  Pallas kernels  140 us (92%)
  local copies, waits for them, and re-layouts  12.3 us (8%)
    pallas_call x1, Pallas kernels, fast_device(): pl.pallas_call(whole_block, out_shape=(shape((faces, rows, cols, ch), bf)...  140 us
    unnamed x25, local copies, waits for them, and re-layouts  12.3 us

profile of v4, /device:TPU:0, one launch (start us, length us, event | category | flops | bytes accessed | tf_op | source)
XLA Modules:
  0.0 153.3 jit_solution(6535188089538191123)
XLA Ops:
  0.6 140.3 %shard_map.187 = (bf16[12,32,16,256]{3,2,1,0:T(8,128)(2,1)}, bf16[12,32,16,256]{3,2,1,0:T(8,128)(2,1)}, bf16[12,9,16,32]{3,2,1,0:T(8,128)(2,1)}, f32[2304,256]{1...) custom-call(bf16[12,32,16,256]{3,2,1,0:T(8,128)(2,1)} %bitcast.20, ...), custom_call_target="tpu_custom_call" | custom-call | tf_op jit(solution)/shard_map/pallas_call | solution.py:1408
  140.9 0.0 copy-start
  140.9 3.9 %copy.30 = bf16[1,12,32,16,256]{4,3,2,1,0:T(8,128)(2,1)} copy(bf16[1,12,32,16,256]{4,3,2,1,0:T(8,128)(2,1)} %bitcast.19) | data formatting | bytes 6291456
  144.9 0.0 copy-done
  144.9 0.0 copy-start.3
  144.9 0.0 copy-start.1
  144.9 1.7 %copy.31 = bf16[1,12,32,16,256]{4,3,2,1,0:T(8,128)(2,1)} copy(bf16[1,12,32,16,256]{4,3,2,1,0:T(8,128)(2,1)S(1)} %bitcast.18) | data formatting | bytes 6291456
  146.5 0.0 copy-done.3
  146.5 0.0 copy-start.2
  146.5 0.8 copy.32
  147.3 0.7 copy-done.1
  148.0 1.5 copy.33
  149.5 0.0 copy-done.7
  149.5 0.0 copy-start.4
  149.5 0.0 copy-start.5
  149.5 0.6 copy.34
  150.0 0.0 copy-done.2
  150.0 1.4 copy.35
  151.4 0.0 copy-done.6
  151.4 0.6 copy.36
  152.0 0.0 copy-done.4
  152.0 0.7 copy.37
  152.7 0.0 copy-done.5
  152.7 0.6 copy.38
  (2 shorter events, 0.0 us)
Async XLA Ops:
  140.9 3.9 %copy-start = (bf16[12,32,16,256]{3,2,1,0:T(8,128)(2,1)S(1)}, bf16[12,32,16,256]{3,2,1,0:T(8,128)(2,1)}, u32[]{:S(2)}) copy-start(bf16[12,32,16,256]{3,2,1,0:T(8,128)(2,1)} %get-tuple-element.19) | copy-start | bytes 9437188
  144.9 1.7 %copy-start.3 = (bf16[12,9,16,32]{3,2,1,0:T(8,128)(2,1)S(1)}, bf16[12,9,16,32]{3,2,1,0:T(8,128)(2,1)}, u32[]{:S(2)}) copy-start(bf16[12,9,16,32]{3,2,1,0:T(8,128)(2,1)} %get-tuple-element.20) | copy-start | bytes 331780
  144.9 3.2 %copy-start.1 = (f32[9,265,256]{2,1,0:T(8,128)S(1)}, f32[9,265,256]{2,1,0:T(8,128)}, u32[]{:S(2)}) copy-start(f32[9,265,256]{2,1,0:T(8,128)} %get-tuple-element.21) | copy-start | bytes 7326724
  146.5 2.9 %copy-start.7 = (f32[1,256]{1,0:T(1,128)S(1)}, f32[1,256]{1,0:T(1,128)}, u32[]{:S(2)}) copy-start(f32[1,256]{1,0:T(1,128)} %get-tuple-element.22) | copy-start | bytes 3076
  146.5 3.5 %copy-start.2 = (f32[2304,256]{1,0:T(8,128)S(1)}, f32[2304,256]{1,0:T(8,128)}, u32[]{:S(2)}) copy-start(f32[2304,256]{1,0:T(8,128)} %get-tuple-element.23) | copy-start | bytes 7077892
  149.5 2.0 %copy-start.6 = (f32[1,256]{1,0:T(1,128)S(1)}, f32[1,256]{1,0:T(1,128)}, u32[]{:S(2)}) copy-start(f32[1,256]{1,0:T(1,128)} %get-tuple-element.24) | copy-start | bytes 3076
  149.5 2.5 %copy-start.4 = (f32[265,256]{1,0:T(8,128)S(1)}, f32[265,256]{1,0:T(8,128)}, u32[]{:S(2)}) copy-start(f32[265,256]{1,0:T(8,128)} %get-tuple-element.43) | copy-start | bytes 814084
  149.5 3.3 %copy-start.5 = (f32[1,256]{1,0:T(1,128)S(1)}, f32[1,256]{1,0:T(1,128)}, u32[]{:S(2)}) copy-start(f32[1,256]{1,0:T(1,128)} %get-tuple-element.26) | copy-start | bytes 3076
